TPU v7x, 32 devices: a whole 2x2x4 slice. The times are simulated.
32 devices in a mesh: dp: 16 (over z, y, core), tensor: 2 (over x).
Axes of the slice: x: 2, y: 2, z: 4, core: 2. Of those that a mesh axis runs over, the one named last changes fastest.
Arguments:
- tokens: bfloat16 [8192, 1024], P(('dp', 'tensor')), may hold values from -6 to 6
- lengths: int32 [32], P(('dp', 'tensor')), may hold values from 64 to 256, as said below
- cotangent: bfloat16 [8192, 1024], P(('dp', 'tensor')), may hold values from -6 to 6
- norm_gain: float32 [1024], replicated, may hold values from 0.5 to 1.5
- w_query: bfloat16 [1024, 512], P(None, 'tensor'), may hold values from -0.1875 to 0.1875
- w_key: bfloat16 [1024, 128], replicated, may hold values from -0.1875 to 0.1875
- w_value: bfloat16 [1024, 128], replicated, may hold values from -0.1875 to 0.1875
- w_gate_z: bfloat16 [1024, 1536], P(None, 'tensor'), may hold values from -0.1875 to 0.1875
- w_ssm_x: bfloat16 [1024, 1536], P(None, 'tensor'), may hold values from -0.1875 to 0.1875
- w_ssm_b: bfloat16 [1024, 128], replicated, may hold values from -0.1875 to 0.1875
- w_ssm_c: bfloat16 [1024, 128], replicated, may hold values from -0.1875 to 0.1875
- w_step: bfloat16 [1024, 24], P(None, 'tensor'), may hold values from -0.1875 to 0.1875
- conv_x_weight: float32 [4, 1536], P(None, 'tensor'), may hold values from -3 to 3
- conv_x_bias: float32 [1536], P('tensor'), may hold values from -0.5 to 0.5
- conv_bc_weight: float32 [4, 256], replicated, may hold values from -3 to 3
- conv_bc_bias: float32 [256], replicated, may hold values from -0.5 to 0.5
- step_bias: float32 [24], P('tensor'), may hold values from -6.9 to -2.3
- decay_log: float32 [24], P('tensor'), may hold values from 0 to 2.77
- skip_gain: float32 [24], P('tensor'), may hold values from 0.5 to 1.5
- ssm_norm_gain: float32 [1536], P('tensor'), may hold values from 0.5 to 1.5
- w_out_att: bfloat16 [512, 1024], P('tensor'), may hold values from -0.75 to 0.75
- w_out_ssm: bfloat16 [1536, 1024], P('tensor'), may hold values from -0.15625 to 0.15625
- ffn_norm_gain: float32 [1024], replicated, may hold values from 0.5 to 1.5
- w_gate: bfloat16 [1024, 2048], P(None, 'tensor'), may hold values from -0.1875 to 0.1875
- w_up: bfloat16 [1024, 2048], P(None, 'tensor'), may hold values from -0.1875 to 0.1875
- w_down: bfloat16 [2048, 1024], P('tensor'), may hold values from -0.125 to 0.125
Outputs:
- layer_output: bfloat16 [8192, 1024], P(('dp', 'tensor'))
- grad_input: float32 [8192, 1024], P(('dp', 'tensor'))
- grad_norm_gain: float32 [1024], replicated
- grad_w_query: float32 [1024, 512], P(None, 'tensor')
- grad_w_key: float32 [1024, 128], replicated
- grad_w_value: float32 [1024, 128], replicated
- grad_w_gate_z: float32 [1024, 1536], P(None, 'tensor')
- grad_w_ssm_x: float32 [1024, 1536], P(None, 'tensor')
- grad_w_ssm_b: float32 [1024, 128], replicated
- grad_w_ssm_c: float32 [1024, 128], replicated
- grad_w_step: float32 [1024, 24], P(None, 'tensor')
- grad_conv_x_weight: float32 [4, 1536], P(None, 'tensor')
- grad_conv_x_bias: float32 [1536], P('tensor')
- grad_conv_bc_weight: float32 [4, 256], replicated
- grad_conv_bc_bias: float32 [256], replicated
- grad_step_bias: float32 [24], P('tensor')
- grad_decay_log: float32 [24], P('tensor')
- grad_skip_gain: float32 [24], P('tensor')
- grad_ssm_norm_gain: float32 [1536], P('tensor')
- grad_w_out_att: float32 [512, 1024], P('tensor')
- grad_w_out_ssm: float32 [1536, 1024], P('tensor')
- grad_ffn_norm_gain: float32 [1024], replicated
- grad_w_gate: float32 [1024, 2048], P(None, 'tensor')
- grad_w_up: float32 [1024, 2048], P(None, 'tensor')
- grad_w_down: float32 [2048, 1024], P('tensor')
Inputs may be any that keep to these rules, and one draw needn't show every extreme that they name: Tokens of a sequence fill its first lengths slots; the rest are padding. Some sequence has exactly 256 tokens and some exactly 64.
All inputs are finite; a program needn't handle non-finite values.
Results may differ from a plain program's by a relative error of at most 0.029.
Values may be sent and summed in bfloat16 or wider, within the bound.
A program may use at most 192 MiB of HBM per device.

v0:
```python
import jax
import jax.numpy as jnp
from jax import lax
from jax.sharding import PartitionSpec as P

HEADS = 8
KV_HEADS = 2
HEAD_DIM = 64
SSM_HEADS = 24
SSM_DIM = 64
SPAN = 128


EPSILON = 1e-05
ROPE_BASE = 100000000000.0
HIGHEST = lax.Precision.HIGHEST


def rms_norm(values, gain):
    return values * lax.rsqrt(jnp.mean(values * values, axis=-1, keepdims=True) + EPSILON) * gain


def rope_turn(values, positions):
    head_width = values.shape[-1]
    half_width = head_width // 2
    freqs = ROPE_BASE ** (-(jnp.arange(half_width).astype(jnp.float32) * 2.0 / head_width))
    angles = positions[:, None] * freqs[None, :]
    cosine = jnp.cos(angles)[:, None, :]
    sine = jnp.sin(angles)[:, None, :]
    first_half = values[..., :half_width]
    second_half = values[..., half_width:]
    return jnp.concatenate(
        [first_half * cosine - second_half * sine, second_half * cosine + first_half * sine],
        axis=-1,
    )


def causal_conv(values, weight, bias):
    taps = weight.shape[0]
    seq_steps = values.shape[0]
    padded = jnp.pad(values, ((taps - 1, 0), (0, 0)))
    total = bias[None, :] + jnp.zeros_like(values)
    for offset in range(taps):
        total = total + weight[offset][None, :] * padded[offset : offset + seq_steps]
    return total


def ssd_scan(inputs, step_sizes, rate_vec, in_map, out_map):
    seq_steps, num_heads, head_width = inputs.shape
    state_size = in_map.shape[1]
    blocks = seq_steps // SPAN
    log_decay = (-(step_sizes * rate_vec[None, :])).reshape(blocks, SPAN, num_heads)
    cumulative = jnp.cumsum(log_decay, axis=1)
    weighted = (inputs * step_sizes[:, :, None]).reshape(blocks, SPAN, num_heads, head_width)
    in_blocks = in_map.reshape(blocks, SPAN, state_size)
    out_blocks = out_map.reshape(blocks, SPAN, state_size)
    lower_mask = (jnp.arange(SPAN)[:, None] >= jnp.arange(SPAN)[None, :])[None, :, :, None]
    differ = cumulative[:, :, None, :] - cumulative[:, None, :, :]
    decay_mat = jnp.where(lower_mask, jnp.exp(jnp.where(lower_mask, differ, 0.0)), 0.0)
    affinity = jnp.einsum("cin,cjn->cij", out_blocks, in_blocks, preferred_element_type=jnp.float32)
    inner_part = jnp.einsum(
        "cijh,cjhp->cihp", affinity[:, :, :, None] * decay_mat, weighted, precision=HIGHEST
    )
    last_log = cumulative[:, -1, :]
    to_end = jnp.exp(last_log[:, None, :] - cumulative)
    block_states = jnp.einsum(
        "cjhp,cjn->chpn", weighted * to_end[:, :, :, None], in_blocks, precision=HIGHEST
    )

    def carry_step(carried, scan_item):
        block_log, block_state = scan_item
        return (jnp.exp(block_log)[:, None, None] * carried + block_state, carried)

    start_state = jnp.zeros((num_heads, head_width, state_size), jnp.float32)
    _, entering = lax.scan(carry_step, start_state, (last_log, block_states))
    outer_part = (
        jnp.einsum("cin,chpn->cihp", out_blocks, entering, precision=HIGHEST)
        * jnp.exp(cumulative)[:, :, :, None]
    )
    return (inner_part + outer_part).reshape(seq_steps, num_heads, head_width)


def contract_rows(left, right):
    return lax.dot_general(
        left, right, (((0,), (0,)), ((), ())), preferred_element_type=jnp.float32
    )


def times_transposed(left, right):
    return lax.dot_general(
        left, right, (((1,), (1,)), ((), ())), preferred_element_type=jnp.float32
    )


def shared_piece(projected, positions, conv_weight, conv_bias):
    kv_width = KV_HEADS * HEAD_DIM
    seq_steps = projected.shape[0]
    turned = rope_turn(
        projected[:, :kv_width].reshape(seq_steps, KV_HEADS, HEAD_DIM), positions
    ).reshape(seq_steps, kv_width)
    mapped = jax.nn.silu(causal_conv(projected[:, 2 * kv_width :], conv_weight, conv_bias))
    return jnp.concatenate([turned, projected[:, kv_width : 2 * kv_width], mapped], axis=1)


def masked_scores(queries, key_sel, key_mask):
    seq_steps = queries.shape[0]
    scores = jnp.einsum(
        "qhd,khd->hqk", queries, key_sel, preferred_element_type=jnp.float32
    ) * HEAD_DIM ** (-0.5)
    allowed = (jnp.arange(seq_steps)[:, None] >= jnp.arange(seq_steps)[None, :]) & (
        key_mask[None, :] > 0.5
    )
    return jnp.where(allowed[None], scores, -1e30)


def attend_forward(queries, keys, values, key_mask, selector):
    key_sel = jnp.einsum("lkd,hk->lhd", keys, selector, preferred_element_type=jnp.float32).astype(
        jnp.bfloat16
    )
    value_sel = jnp.einsum(
        "lkd,hk->lhd", values, selector, preferred_element_type=jnp.float32
    ).astype(jnp.bfloat16)
    scores = masked_scores(queries, key_sel, key_mask)
    top_score = jnp.max(scores, axis=-1, keepdims=True)
    log_total = top_score + jnp.log(jnp.sum(jnp.exp(scores - top_score), axis=-1, keepdims=True))
    softmaxed = jnp.exp(scores - log_total)
    outputs = jnp.einsum(
        "hqk,khd->qhd",
        softmaxed.astype(jnp.bfloat16),
        value_sel,
        preferred_element_type=jnp.float32,
    )
    return (outputs, log_total[..., 0])


def attend_backward(queries, keys, values, key_mask, selector, log_total, grad_out):
    key_sel = jnp.einsum("lkd,hk->lhd", keys, selector, preferred_element_type=jnp.float32).astype(
        jnp.bfloat16
    )
    value_sel = jnp.einsum(
        "lkd,hk->lhd", values, selector, preferred_element_type=jnp.float32
    ).astype(jnp.bfloat16)
    softmaxed = jnp.exp(masked_scores(queries, key_sel, key_mask) - log_total[..., None])
    grad_prob = jnp.einsum("qhd,khd->hqk", grad_out, value_sel, preferred_element_type=jnp.float32)
    grad_score = (
        softmaxed * (grad_prob - jnp.sum(softmaxed * grad_prob, axis=-1, keepdims=True))
    ).astype(jnp.bfloat16)
    scale = HEAD_DIM ** (-0.5)
    grad_query = (
        jnp.einsum("hqk,khd->qhd", grad_score, key_sel, preferred_element_type=jnp.float32) * scale
    )
    grad_key_sel = (
        jnp.einsum("hqk,qhd->khd", grad_score, queries, preferred_element_type=jnp.float32) * scale
    )
    grad_value_sel = jnp.einsum(
        "hqk,qhd->khd", softmaxed.astype(jnp.bfloat16), grad_out, preferred_element_type=jnp.float32
    )
    selector_f = selector.astype(jnp.float32)
    grad_key = jnp.einsum("lhd,hk->lkd", grad_key_sel, selector_f, precision=HIGHEST)
    grad_value = jnp.einsum("lhd,hk->lkd", grad_value_sel, selector_f, precision=HIGHEST)
    return (grad_query, grad_key, grad_value)


def on_device(
    tokens,
    lengths,
    cotangent,
    norm_gain,
    w_query,
    w_key,
    w_value,
    w_gate_z,
    w_ssm_x,
    w_ssm_b,
    w_ssm_c,
    w_step,
    conv_x_weight,
    conv_x_bias,
    conv_bc_weight,
    conv_bc_bias,
    step_bias,
    decay_log,
    skip_gain,
    ssm_norm_gain,
    w_out_att,
    w_out_ssm,
    ffn_norm_gain,
    w_gate,
    w_up,
    w_down,
):
    seq_len = tokens.shape[0]
    groups = lax.axis_size("tensor")
    position = lax.axis_index("tensor")
    total_rows = seq_len * groups
    heads_here = w_query.shape[1] // HEAD_DIM
    ssm_here = w_gate_z.shape[1] // SSM_DIM
    kv_width = w_key.shape[1]
    state_size = w_ssm_b.shape[1]
    ssm_width_all = SSM_HEADS * SSM_DIM
    own_pos = jnp.arange(seq_len).astype(jnp.float32)
    own_mask = (jnp.arange(seq_len) < lengths[0]).astype(jnp.float32)
    own_flags = own_mask.astype(jnp.bfloat16)
    inputs = tokens.astype(jnp.float32)
    normed, norm_pull = jax.vjp(rms_norm, inputs, norm_gain)
    first_normed = normed.astype(jnp.bfloat16)
    shared_w = jnp.concatenate([w_key, w_value, w_ssm_b, w_ssm_c], axis=1)

    def shared_part(projected, conv_weight, conv_bias):
        return shared_piece(projected, own_pos, conv_weight, conv_bias)

    gathered, flags_all = (
        lax.all_gather(first_normed, "tensor", axis=0, tiled=True),
        lax.all_gather(own_flags, "tensor", axis=0, tiled=True),
    )
    shared_all = jnp.dot(gathered, shared_w, preferred_element_type=jnp.float32)
    shared_vals = (
        jax.vmap(shared_part, in_axes=(0, None, None))(
            shared_all.reshape(groups, seq_len, -1), conv_bc_weight, conv_bc_bias
        )
        .reshape(total_rows, -1)
        .astype(jnp.bfloat16)
    )
    own_proj = lax.dynamic_slice_in_dim(shared_all, position * seq_len, seq_len, 0)
    key_mask_all = flags_all.astype(jnp.float32).reshape(groups, seq_len)
    query_proj = jnp.dot(gathered, w_query, preferred_element_type=jnp.float32).reshape(
        groups, seq_len, heads_here, HEAD_DIM
    )
    query_turned = jax.vmap(rope_turn, in_axes=(0, None))(query_proj, own_pos).astype(jnp.bfloat16)
    key_turned = shared_vals[:, :kv_width].reshape(groups, seq_len, KV_HEADS, HEAD_DIM)
    value_vals = shared_vals[:, kv_width : 2 * kv_width].reshape(
        groups, seq_len, KV_HEADS, HEAD_DIM
    )
    in_map = shared_vals[:, 2 * kv_width : 2 * kv_width + state_size].astype(jnp.float32)
    out_map = shared_vals[:, 2 * kv_width + state_size :].astype(jnp.float32)
    head_ids = position * heads_here + jnp.arange(heads_here)
    selector = ((head_ids // (HEADS // KV_HEADS))[:, None] == jnp.arange(KV_HEADS)[None, :]).astype(
        jnp.bfloat16
    )

    def forward_one(packed):
        return attend_forward(packed[0], packed[1], packed[2], packed[3], selector)

    att_out, log_totals = lax.map(forward_one, (query_turned, key_turned, value_vals, key_mask_all))
    mix_att = att_out.reshape(total_rows, heads_here * HEAD_DIM).astype(jnp.bfloat16)
    z_proj = jnp.dot(gathered, w_gate_z, preferred_element_type=jnp.float32)
    x_proj = jnp.dot(gathered, w_ssm_x, preferred_element_type=jnp.float32)
    step_proj = jnp.dot(gathered, w_step, preferred_element_type=jnp.float32)

    def seq_view(array_in):
        return array_in.reshape(groups, seq_len, array_in.shape[-1])

    def ssm_piece(
        x_vals,
        z_vals,
        step_vals,
        in_vals,
        out_vals,
        conv_weight,
        conv_bias,
        bias_step,
        log_rate,
        skip_vec,
    ):
        conv_out = jax.nn.silu(
            jax.vmap(causal_conv, in_axes=(0, None, None))(seq_view(x_vals), conv_weight, conv_bias)
        )
        step_sizes = jax.nn.softplus(seq_view(step_vals) + bias_step) * key_mask_all[:, :, None]
        heads_view = conv_out.reshape(groups, seq_len, ssm_here, SSM_DIM)
        scanned = jax.vmap(ssd_scan, in_axes=(0, 0, None, 0, 0))(
            heads_view, step_sizes, jnp.exp(log_rate), seq_view(in_vals), seq_view(out_vals)
        )
        result_y = scanned + skip_vec[None, None, :, None] * heads_view
        return result_y.reshape(total_rows, ssm_here * SSM_DIM) * jax.nn.silu(z_vals)

    gated, ssm_pull = jax.vjp(
        ssm_piece,
        x_proj,
        z_proj,
        step_proj,
        in_map,
        out_map,
        conv_x_weight,
        conv_x_bias,
        step_bias,
        decay_log,
        skip_gain,
    )
    square_sums = lax.psum(jnp.sum(gated * gated, axis=1), "tensor")
    inv_scale = lax.rsqrt(square_sums / ssm_width_all + EPSILON)[:, None]
    mix_ssm = (gated * inv_scale * ssm_norm_gain).astype(jnp.bfloat16)
    branch = lax.psum_scatter(
        jnp.dot(mix_att, w_out_att, preferred_element_type=jnp.float32)
        + jnp.dot(mix_ssm, w_out_ssm, preferred_element_type=jnp.float32),
        "tensor",
        scatter_dimension=0,
        tiled=True,
    )
    resid = inputs + branch
    normed_two, norm_two_pull = jax.vjp(rms_norm, resid, ffn_norm_gain)
    second_normed = normed_two.astype(jnp.bfloat16)
    second_all = lax.all_gather(second_normed, "tensor", axis=0, tiled=True)
    gate_vals = jnp.dot(second_all, w_gate, preferred_element_type=jnp.float32)
    up_vals = jnp.dot(second_all, w_up, preferred_element_type=jnp.float32)
    sigma_gate = jax.nn.sigmoid(gate_vals)
    silu_gate = gate_vals * sigma_gate
    hidden = (silu_gate * up_vals).astype(jnp.bfloat16)
    ffn_result = lax.psum_scatter(
        jnp.dot(hidden, w_down, preferred_element_type=jnp.float32).astype(jnp.bfloat16),
        "tensor",
        scatter_dimension=0,
        tiled=True,
    ).astype(jnp.float32)
    layer_output = (resid + ffn_result).astype(jnp.bfloat16)
    cot_rows = cotangent.astype(jnp.float32) * own_mask[:, None]
    cot_all = lax.all_gather(cot_rows.astype(jnp.bfloat16), "tensor", axis=0, tiled=True)
    d_hidden = times_transposed(cot_all, w_down).astype(jnp.bfloat16).astype(jnp.float32)
    grad_down = contract_rows(hidden, cot_all)
    d_gate = (d_hidden * up_vals * (sigma_gate * (1.0 + gate_vals * (1.0 - sigma_gate)))).astype(
        jnp.bfloat16
    )
    d_up = (d_hidden * silu_gate).astype(jnp.bfloat16)
    grad_gate = contract_rows(second_all, d_gate)
    grad_up = contract_rows(second_all, d_up)
    d_second = lax.psum_scatter(
        times_transposed(d_gate, w_gate) + times_transposed(d_up, w_up),
        "tensor",
        scatter_dimension=0,
        tiled=True,
    )
    d_resid_norm, grad_ffn_gain = norm_two_pull(d_second)
    d_resid = cot_rows + d_resid_norm
    d_branch_all = lax.all_gather(d_resid.astype(jnp.bfloat16), "tensor", axis=0, tiled=True)
    grad_out_att = contract_rows(mix_att, d_branch_all)
    grad_out_ssm = contract_rows(mix_ssm, d_branch_all)
    d_att = times_transposed(d_branch_all, w_out_att).astype(jnp.bfloat16)
    d_mix = times_transposed(d_branch_all, w_out_ssm).astype(jnp.bfloat16).astype(jnp.float32)
    scaled_grad = d_mix * ssm_norm_gain
    back_sums = lax.psum(jnp.sum(scaled_grad * gated, axis=1), "tensor")
    d_gated = inv_scale * scaled_grad - gated * inv_scale**3 * (back_sums / ssm_width_all)[:, None]
    grad_ssm_gain = jnp.sum(d_mix * gated * inv_scale, axis=0)
    (
        d_x_proj,
        d_z_proj,
        d_step_proj,
        d_in_map,
        d_out_map,
        grad_conv_x_weight,
        grad_conv_x_bias,
        grad_step_bias,
        grad_decay_log,
        grad_skip_gain,
    ) = ssm_pull(d_gated)
    d_x_low = d_x_proj.astype(jnp.bfloat16)
    d_z_low = d_z_proj.astype(jnp.bfloat16)
    d_step_low = d_step_proj.astype(jnp.bfloat16)

    def backward_one(packed):
        return attend_backward(
            packed[0], packed[1], packed[2], packed[3], selector, packed[4], packed[5]
        )

    grad_att_out = d_att.reshape(groups, seq_len, heads_here, HEAD_DIM)
    grad_q_turned, grad_k_turned, grad_v_vals = lax.map(
        backward_one, (query_turned, key_turned, value_vals, key_mask_all, log_totals, grad_att_out)
    )
    d_query = (
        jax.vmap(rope_turn, in_axes=(0, None))(grad_q_turned, -own_pos)
        .reshape(total_rows, heads_here * HEAD_DIM)
        .astype(jnp.bfloat16)
    )
    grad_query = contract_rows(gathered, d_query)
    grad_gate_z = contract_rows(gathered, d_z_low)
    grad_ssm_x = contract_rows(gathered, d_x_low)
    grad_step = contract_rows(gathered, d_step_low)
    d_first_terms = (
        times_transposed(d_query, w_query)
        + times_transposed(d_z_low, w_gate_z)
        + times_transposed(d_x_low, w_ssm_x)
        + times_transposed(d_step_low, w_step)
    )
    d_shared_all = jnp.concatenate(
        [
            grad_k_turned.reshape(total_rows, kv_width),
            grad_v_vals.reshape(total_rows, kv_width),
            d_in_map,
            d_out_map,
        ],
        axis=1,
    )
    d_first_own, d_shared_own = (
        lax.psum_scatter(
            d_first_terms.astype(jnp.bfloat16), "tensor", scatter_dimension=0, tiled=True
        ).astype(jnp.float32),
        lax.psum_scatter(
            d_shared_all.astype(jnp.bfloat16), "tensor", scatter_dimension=0, tiled=True
        ).astype(jnp.float32),
    )
    _, shared_pull = jax.vjp(shared_part, own_proj, conv_bc_weight, conv_bc_bias)
    d_own_proj, grad_conv_bc_weight, grad_conv_bc_bias = shared_pull(d_shared_own)
    d_own_low = d_own_proj.astype(jnp.bfloat16)
    grad_shared_w = contract_rows(first_normed, d_own_low)
    d_first = d_first_own + times_transposed(d_own_low, shared_w)
    d_input_norm, grad_norm_gain = norm_pull(d_first)
    grad_input = d_resid + d_input_norm
    grad_key = grad_shared_w[:, :kv_width]
    grad_value = grad_shared_w[:, kv_width : 2 * kv_width]
    grad_in_map = grad_shared_w[:, 2 * kv_width : 2 * kv_width + state_size]
    grad_out_map = grad_shared_w[:, 2 * kv_width + state_size :]
    data_grads = (
        lax.psum(grad_query.astype(jnp.bfloat16), "dp").astype(jnp.float32),
        lax.psum(grad_gate_z.astype(jnp.bfloat16), "dp").astype(jnp.float32),
        lax.psum(grad_ssm_x.astype(jnp.bfloat16), "dp").astype(jnp.float32),
        lax.psum(grad_step.astype(jnp.bfloat16), "dp").astype(jnp.float32),
        lax.psum(grad_conv_x_weight.astype(jnp.bfloat16), "dp").astype(jnp.float32),
        lax.psum(grad_conv_x_bias.astype(jnp.bfloat16), "dp").astype(jnp.float32),
        lax.psum(grad_step_bias.astype(jnp.bfloat16), "dp").astype(jnp.float32),
        lax.psum(grad_decay_log.astype(jnp.bfloat16), "dp").astype(jnp.float32),
        lax.psum(grad_skip_gain.astype(jnp.bfloat16), "dp").astype(jnp.float32),
        lax.psum(grad_ssm_gain.astype(jnp.bfloat16), "dp").astype(jnp.float32),
        lax.psum(grad_out_att.astype(jnp.bfloat16), "dp").astype(jnp.float32),
        lax.psum(grad_out_ssm.astype(jnp.bfloat16), "dp").astype(jnp.float32),
        lax.psum(grad_gate.astype(jnp.bfloat16), "dp").astype(jnp.float32),
        lax.psum(grad_up.astype(jnp.bfloat16), "dp").astype(jnp.float32),
        lax.psum(grad_down.astype(jnp.bfloat16), "dp").astype(jnp.float32),
    )
    shared_grads = lax.psum(
        (
            grad_key,
            grad_value,
            grad_in_map,
            grad_out_map,
            grad_conv_bc_weight,
            grad_conv_bc_bias,
            grad_norm_gain,
            grad_ffn_gain,
        ),
        ("dp", "tensor"),
    )
    return (
        layer_output,
        grad_input,
        shared_grads[6],
        data_grads[0],
        shared_grads[0],
        shared_grads[1],
        data_grads[1],
        data_grads[2],
        shared_grads[2],
        shared_grads[3],
        data_grads[3],
        data_grads[4],
        data_grads[5],
        shared_grads[4],
        shared_grads[5],
        data_grads[6],
        data_grads[7],
        data_grads[8],
        data_grads[9],
        data_grads[10],
        data_grads[11],
        shared_grads[7],
        data_grads[12],
        data_grads[13],
        data_grads[14],
    )


def solution(mesh):
    placed = (
        P(("dp", "tensor"), None),
        P(("dp", "tensor")),
        P(("dp", "tensor"), None),
        P(),
        P(None, "tensor"),
        P(),
        P(),
        P(None, "tensor"),
        P(None, "tensor"),
        P(),
        P(),
        P(None, "tensor"),
        P(None, "tensor"),
        P("tensor"),
        P(),
        P(),
        P("tensor"),
        P("tensor"),
        P("tensor"),
        P("tensor"),
        P("tensor", None),
        P("tensor", None),
        P(),
        P(None, "tensor"),
        P(None, "tensor"),
        P("tensor", None),
    )
    return jax.shard_map(
        on_device,
        mesh=mesh,
        in_specs=placed,
        out_specs=(
            P(("dp", "tensor"), None),
            P(("dp", "tensor"), None),
            P(),
            P(None, "tensor"),
            P(),
            P(),
            P(None, "tensor"),
            P(None, "tensor"),
            P(),
            P(),
            P(None, "tensor"),
            P(None, "tensor"),
            P("tensor"),
            P(),
            P(),
            P("tensor"),
            P("tensor"),
            P("tensor"),
            P("tensor"),
            P("tensor", None),
            P("tensor", None),
            P(),
            P(None, "tensor"),
            P(None, "tensor"),
            P("tensor", None),
        ),
        check_vma=False,
    )
```

profile of v0, /device:TPU:0, one launch (start us, length us, event | category | flops | bytes accessed | tf_op | source)
XLA Modules:
  0.0 843.6 jit_solution(17856076924392298710)
XLA Ops:
  12.3 5.1 all-gather
  22.2 12.8 %all-gather.6.cloned.1.call-done = bf16[512,1024]{1,0:T(8,128)(2,1)} async-done(((bf16[256,1024]{1,0:T(8,128)(2,1)}), bf16[512,1024]{1,0:T(8,128)(2,1)}) %all-gather.6.cloned.1.call-update) | async-done | bytes 1048592 | tf_op jit(solution)/shard_map/all_gather | solution.py:213
  46.0 5.9 fusion.109
  71.7 6.0 while.70
  81.4 6.3 bitcast_add_fusion.3
  96.8 5.2 multiply_reduce_fusion.7
  119.7 8.0 while.68
  136.5 29.3 %reduce-scatter.6.cloned.1.call-done = f32[256,1024]{1,0:T(8,128)} async-done(((f32[512,1024]{1,0:T(8,128)}), f32[256,1024]{1,0:T(8,128)}) %reduce-scatter.6.cloned.1.call-update) | async-done | bytes 1048592 | tf_op jit(solution)/shard_map/reduce_scatter | solution.py:292
  170.4 18.9 %all-gather.10.cloned.1.call-done = bf16[512,1024]{1,0:T(8,128)(2,1)} async-done(((bf16[256,1024]{1,0:T(8,128)(2,1)}), bf16[512,1024]{1,0:T(8,128)(2,1)}) %all-gather.10.cloned.1.call-update) | async-done | bytes 1048592 | tf_op jit(solution)/shard_map/all_gather | solution.py:316
  193.5 19.2 %all-gather.8.cloned.1.call-done = bf16[512,1024]{1,0:T(8,128)(2,1)} async-done(((bf16[256,1024]{1,0:T(8,128)(2,1)}), bf16[512,1024]{1,0:T(8,128)(2,1)}) %all-gather.8.cloned.1.call-update) | async-done | bytes 1048592 | tf_op jit(solution)/shard_map/all_gather | solution.py:302
  228.2 26.9 %reduce-scatter.10.cloned.1.call-done = f32[256,1024]{1,0:T(8,128)} async-done(((f32[512,1024]{1,0:T(8,128)}), f32[256,1024]{1,0:T(8,128)}) %reduce-scatter.10.cloned.1.call-update) | async-done | bytes 1048592 | tf_op jit(solution)/shard_map/reduce_scatter | solution.py:325
  258.5 19.0 %reduce-scatter.8.cloned.1.call-done = bf16[256,1024]{1,0:T(8,128)(2,1)} async-done(((bf16[512,1024]{1,0:T(8,128)(2,1)}), bf16[256,1024]{1,0:T(8,128)(2,1)}) %reduce-scatter.8.cloned.1.call-update) | async-done | bytes 524304 | tf_op jit(solution)/shard_map/reduce_scatter | solution.py:308
  286.9 15.0 %all-gather.12.cloned.1.call-done = bf16[512,1024]{1,0:T(8,128)(2,1)} async-done(((bf16[256,1024]{1,0:T(8,128)(2,1)}), bf16[512,1024]{1,0:T(8,128)(2,1)}) %all-gather.12.cloned.1.call-update) | async-done | bytes 1048592 | tf_op jit(solution)/shard_map/all_gather | solution.py:333
  305.9 5.3 psum.176
  328.3 6.4 while.71
  337.9 8.0 fusion.85
  353.7 5.4 fusion.136
  374.9 5.4 reduce_window_sum.23
  386.2 17.5 %while.69 = (s32[]{:T(128)}, f32[2,256,4,64]{1,3,2,0:T(8,128)}, bf16[2,256,2,64]{1,2,3,0:T(2,128)(2,1)}, bf16[2,256,2,64]{1,2,3,0:T(2,128)(2,1)}, bf16[2,256,2,6...) while((s32[]{:T(128)}, f32[2,256,4,64]{1,3,2,0:T(8,128)}, ...), condition=%wide.region_17.18_spmd.clone.clone, body=%wide.region_15.17_spmd.clone.sunk.clone | while | flops 174193984 | bytes 17195856 | solution.py:364
  411.0 5.1 multiply_reduce_fusion.4
  452.8 63.3 %all-reduce.27 = (bf16[1024,12]{0,1:T(8,128)(2,1)S(1)}, bf16[4,768]{1,0:T(4,128)(2,1)S(1)}, bf16[768]{0:T(1024)(128)(2,1)S(1)}, bf16[12]{0:T(256)(128)(2,1)S(1)}...) all-reduce(bf16[1024,12]{0,1:T(8,128)(2,1)S(1)} %copy-done.88, ...), channel_id=1, replica_groups=mesh['dp'=16,'tensor'=2] {'dp'}, use_global_device_ids=true, to_apply=%region_43.44 | all-reduce | flops 16932 | bytes 67728 | tf_op jit(solution)/shard_map/psum | solution.py:414
  522.4 38.2 %all-reduce.25 = (f32[1024]{0:T(1024)}, f32[4,256]{1,0:T(4,128)}, f32[256]{0:T(256)}, f32[1024]{0:T(1024)}) all-reduce(f32[1024]{0:T(1024)S(1)} %get-tuple-element.614, f32[4,256]{1,0:T(4,128)S(1)} %pad_add_fusion.7, f32[256]{0:T(256)S(1)} %copy-done.149, f32[1024]{0:T(1024)S(1)} %copy-done.124), channel_id=1, replica_groups=mesh['dp'=16,'tensor'=2] {'dp','tensor'}, use_global_device_ids=true, to_apply=%region_35.36 | all-reduce | flops 3328 | bytes 26624 | tf_op jit(solution)/shard_map/psum | solution.py:427
  561.9 128.1 %all-reduce.34.cloned.1.call-done = (bf16[1024,256]{1,0:T(8,128)(2,1)}, bf16[1024,768]{1,0:T(8,128)(2,1)}, bf16[1024,768]{1,0:T(8,128)(2,1)}, bf16[256,1024]{1,0...) async-done(((bf16[1024,256]{1,0:T(8,128)(2,1)}, bf16[1024,768]{1,0:T(8,128)(2,1)}, ...) | async-done | bytes 12058640 | tf_op jit(solution)/shard_map/psum | solution.py:411
  707.5 123.8 %all-reduce.32.cloned.1.call-done = (f32[1024,128]{1,0:T(8,128)}, f32[1024,128]{1,0:T(8,128)}, f32[1024,128]{1,0:T(8,128)}, f32[1024,128]{1,0:T(8,128)}) async-done(((f32[1024,128]{1,0:T(8,128)}, f32[1024,128]{1,0:T(8,128)}, f32[1024,128]{1,0:T(8,128)}, f32[1024,128]{1,0:T(8,128)}), (f32[1024,128]{1,0:T(8,128)}, f32[1024,128]{1,0:T(8,128)}, f32[1024,128]{1,0:T(8,128)}, ...) | async-done | bytes 2097168 | tf_op jit(solution)/shard_map/psum | solution.py:427
  (639 shorter events, 280.2 us)
Async XLA Ops:
  7.2 208.8 %copy-start = (bf16[1024,1024]{1,0:T(8,128)(2,1)S(1)}, bf16[1024,1024]{1,0:T(8,128)(2,1)}, u32[]{:S(2)}) copy-start(bf16[1024,1024]{1,0:T(8,128)(2,1)} %param.58) | copy-start | bytes 6291460
  7.3 27.7 %all-gather.6.cloned.1.call-start = ((), (), s32[]{:S(2)}) async-start(), calls=%async_computation.5 | async-start | bytes 1572864 | tf_op jit(solution)/shard_map/all_gather | solution.py:213
  10.8 155.0 %reduce-scatter.6.cloned.1.call-start = ((), (), s32[]{:S(2)}) async-start(), calls=%async_computation.6 | async-start | bytes 3145728 | tf_op jit(solution)/shard_map/reduce_scatter | solution.py:292
  12.2 33.8 %copy-start.100 = (f32[768]{0:T(1024)}, f32[768]{0:T(1024)S(1)}, u32[]{:S(2)}) copy-start(f32[768]{0:T(1024)S(1)} %get-tuple-element.621) | copy-start | bytes 9220
  12.2 33.8 %copy-start.102 = (f32[768]{0:T(1024)}, f32[768]{0:T(1024)S(1)}, u32[]{:S(2)}) copy-start(f32[768]{0:T(1024)S(1)} %get-tuple-element.622) | copy-start | bytes 9220
  21.2 42.2 %copy-start.115 = (f32[1,256]{1,0:T(1,128)}, f32[1,256]{1,0:T(1,128)S(1)}, u32[]{:S(2)}) copy-start(f32[1,256]{1,0:T(1,128)S(1)} %get-tuple-element.774) | copy-start | bytes 3076
  21.2 42.2 %copy-start.117 = (f32[1,256]{1,0:T(1,128)}, f32[1,256]{1,0:T(1,128)S(1)}, u32[]{:S(2)}) copy-start(f32[1,256]{1,0:T(1,128)S(1)} %get-tuple-element.775) | copy-start | bytes 3076
  21.2 42.2 %copy-start.119 = (f32[1,256]{1,0:T(1,128)}, f32[1,256]{1,0:T(1,128)S(1)}, u32[]{:S(2)}) copy-start(f32[1,256]{1,0:T(1,128)S(1)} %get-tuple-element.776) | copy-start | bytes 3076
  21.2 42.2 %copy-start.121 = (f32[1,256]{1,0:T(1,128)}, f32[1,256]{1,0:T(1,128)S(1)}, u32[]{:S(2)}) copy-start(f32[1,256]{1,0:T(1,128)S(1)} %get-tuple-element.777) | copy-start | bytes 3076
  133.8 55.5 %all-gather.10.cloned.1.call-start = ((), (), s32[]{:S(2)}) async-start(), calls=%async_computation.9 | async-start | bytes 1572864 | tf_op jit(solution)/shard_map/all_gather | solution.py:316
  136.5 76.3 %all-gather.8.cloned.1.call-start = ((), (), s32[]{:S(2)}) async-start(), calls=%async_computation.7 | async-start | bytes 1572864 | tf_op jit(solution)/shard_map/all_gather | solution.py:302
  170.2 84.9 %reduce-scatter.10.cloned.1.call-start = ((), (), s32[]{:S(2)}) async-start(), calls=%async_computation.10 | async-start | bytes 3145728 | tf_op jit(solution)/shard_map/reduce_scatter | solution.py:325
  223.0 54.4 %reduce-scatter.8.cloned.1.call-start = ((), (), s32[]{:S(2)}) async-start(), calls=%async_computation.8 | async-start | bytes 1572864 | tf_op jit(solution)/shard_map/reduce_scatter | solution.py:308
  228.1 73.8 %all-gather.12.cloned.1.call-start = ((), (), s32[]{:S(2)}) async-start(), calls=%async_computation.11 | async-start | bytes 1572864 | tf_op jit(solution)/shard_map/all_gather | solution.py:333
  280.5 167.3 %reduce-scatter.14.cloned.1.call-start = ((), (), s32[]{:S(2)}) async-start(), calls=%async_computation.13 | async-start | bytes 786432 | tf_op jit(solution)/shard_map/reduce_scatter | solution.py:395
  410.9 109.3 %reduce-scatter.12.cloned.1.call-start = ((), (), s32[]{:S(2)}) async-start(), calls=%async_computation.12 | async-start | bytes 1572864 | tf_op jit(solution)/shard_map/reduce_scatter | solution.py:392
  428.2 261.8 %all-reduce.34.cloned.1.call-start = ((), (), s32[]{:S(2)}) async-start(), calls=%async_computation.15 | async-start | bytes 24117248 | tf_op jit(solution)/shard_map/psum | solution.py:411
  444.5 386.8 %all-reduce.32.cloned.1.call-start = ((), (), s32[]{:S(2)}) async-start(), calls=%async_computation.14 | async-start | bytes 4194304 | tf_op jit(solution)/shard_map/psum | solution.py:427
  452.1 68.1 %copy-start.16 = (bf16[256,1024]{1,0:T(8,128)(2,1)S(1)}, bf16[256,1024]{1,0:T(8,128)(2,1)}, u32[]{:S(2)}) copy-start(bf16[256,1024]{1,0:T(8,128)(2,1)} %param.34) | copy-start | bytes 1572868
  452.1 68.1 %copy-start.64 = (f32[256,128]{1,0:T(8,128)S(1)}, f32[256,128]{1,0:T(8,128)}, u32[]{:S(2)}) copy-start(f32[256,128]{1,0:T(8,128)} %copy-done.63) | copy-start | bytes 393220
  452.1 68.1 %copy-start.129 = (f32[1024]{0:T(1024)S(1)}, f32[1024]{0:T(1024)}, u32[]{:S(2)}) copy-start(f32[1024]{0:T(1024)} %param.37) | copy-start | bytes 12292
  452.1 68.1 %copy-start.137 = (f32[256]{0:T(256)S(1)}, f32[256]{0:T(256)}, u32[]{:S(2)}) copy-start(f32[256]{0:T(256)} %copy-done.136) | copy-start | bytes 3076
  520.1 40.5 %copy-start.134 = (f32[256]{0:T(256)S(1)}, f32[256]{0:T(256)}, u32[]{:S(2)}) copy-start(f32[256]{0:T(256)} %copy-done.133) | copy-start | bytes 3076
  520.1 40.5 %copy-start.26 = (f32[256,1024]{1,0:T(8,128)S(1)}, f32[256,1024]{1,0:T(8,128)}, u32[]{:S(2)}) copy-start(f32[256,1024]{1,0:T(8,128)} %get-tuple-element.723) | copy-start | bytes 3145732
  (166 other events, 833.9 us)
Sparse Core Ops, SparseCore 0:
  10.9 23.9 all-gather.5
  133.9 31.8 reduce-scatter.5
  168.0 21.2 all-gather.9
  191.4 21.2 all-gather.7
  223.2 31.8 reduce-scatter.9
  257.1 20.3 reduce-scatter.7
  280.6 21.2 all-gather.11
  411.0 14.5 reduce-scatter.13
  428.3 20.3 reduce-scatter.11
  456.7 233.2 all-reduce.33
  697.2 134.1 all-reduce.31
where the time goes:
time: 849 us; the launch traced here: 844 us
  waiting for transfers between devices  393 us (46%)
  matrix products  133 us (16%)
  blocking collectives  117 us (14%)
  local copies, waits for them, and re-layouts  93.1 us (11%)
  other arithmetic  89.6 us (11%)
  between operations  16.7 us (2%)
    psum x1, waiting for transfers between devices, on_device(): lax.psum(grad_query.astype(jnp.bfloat16), 'dp').astype(jnp.float32)  128 us
    psum x1, waiting for transfers between devices, on_device(): lax.psum((grad_key, grad_value, grad_in_map, grad_out_map, grad_conv_bc_w...  124 us
    psum x1, blocking collectives, on_device(): lax.psum(grad_step.astype(jnp.bfloat16), 'dp').astype(jnp.float32)  63.3 us
    psum x1, blocking collectives, on_device(): lax.psum((grad_key, grad_value, grad_in_map, grad_out_map, grad_conv_bc_w...  38.2 us
    reduce_scatter x1, waiting for transfers between devices, on_device(): lax.psum_scatter(jnp.dot(mix_att, w_out_att, preferred_element_type=jnp.f...  29.3 us
    reduce_scatter x1, waiting for transfers between devices, on_device(): lax.psum_scatter(times_transposed(d_gate, w_gate) + times_transposed(d_up...  26.9 us
    unnamed x337, local copies, waits for them, and re-layouts  21.9 us
    dot_general x10, matrix products, contract_rows(): lax.dot_general(left, right, (((0,), (0,)), ((), ())), preferred_element_...  21.7 us
  transfers between devices with their start and end apart: 11, of which 9 were waited for; matrix products, arithmetic and copies ran while one was open for 11% of the time, Pallas kernels for 0%

commit v1 on v0

v1 whole, which is shorter than its diff:
```python
import functools

import jax
import jax.numpy as jnp
from jax import lax
from jax.experimental import pallas as pl
from jax.experimental.pallas import tpu as pltpu
from jax.sharding import PartitionSpec as P

HEADS = 8
KV_HEADS = 2
HEAD_DIM = 64
SSM_HEADS = 24
SSM_DIM = 64
STATE = 128
SPAN = 128
LANES = 128

EPSILON = 1e-05
ROPE_BASE = 100000000000.0
F32 = jnp.float32
BF16 = jnp.bfloat16
VMEM_LIMIT = 50 * 1024 * 1024


def mm(left, right):
    return jnp.dot(left, right, preferred_element_type=F32)


def mm_nt(left, right):
    return lax.dot_general(left, right, (((1,), (1,)), ((), ())), preferred_element_type=F32)


def mm_tn(left, right):
    return lax.dot_general(left, right, (((0,), (0,)), ((), ())), preferred_element_type=F32)


def pieces(values, count):
    terms = []
    for _ in range(count):
        term = values.astype(BF16)
        terms.append(term)
        values = values - term.astype(F32)
    return terms


def sigmoid(values):
    return 1.0 / (1.0 + jnp.exp(-values))


def softplus(values):
    return jnp.maximum(values, 0.0) + jnp.log1p(jnp.exp(-jnp.abs(values)))


def lane_ids(shape):
    return lax.broadcasted_iota(jnp.int32, shape, 1)


def row_ids(shape):
    return lax.broadcasted_iota(jnp.int32, shape, 0)


def repeat_lanes(column, count):
    return jnp.concatenate([column] * count, axis=1) if count > 1 else column


def column_of(row):
    ones = jnp.where(row_ids((16, LANES)) == 0, 1.0, 0.0).astype(BF16)
    total = None
    for term in pieces(row, 3):
        part = mm_tn(term, ones)
        total = part if total is None else total + part
    return total


def row_sums(values):
    ones = jnp.ones((16, values.shape[1]), BF16)
    high, low = pieces(values, 2)
    return mm_nt(ones, high) + mm_nt(ones, low)


def causal_shift(values, steps):
    if steps == 0:
        return values
    rolled = pltpu.roll(values, steps, 0)
    return jnp.where(row_ids(values.shape) >= steps, rolled, 0.0)


def anti_shift(values, steps):
    if steps == 0:
        return values
    length = values.shape[0]
    rolled = pltpu.roll(values, length - steps, 0)
    return jnp.where(row_ids(values.shape) < length - steps, rolled, 0.0)


def conv(values, weight, bias):
    taps = weight.shape[0]
    total = bias + weight[taps - 1 : taps] * values
    for offset in range(taps - 1):
        total = total + weight[offset : offset + 1] * causal_shift(values, taps - 1 - offset)
    return total


def conv_back(grad, values, weight):
    taps = weight.shape[0]
    total, rows = None, []
    for offset in range(taps):
        steps = taps - 1 - offset
        moved = anti_shift(grad, steps)
        part = weight[offset : offset + 1] * moved
        total = part if total is None else total + part
        rows.append(jnp.sum(moved * values, axis=0, keepdims=True))
    rows.append(jnp.sum(grad, axis=0, keepdims=True))
    return total, rows


def rope(values, cosine, sine_first, sine_second):
    ahead = pltpu.roll(values, LANES - HEAD_DIM // 2, 1)
    behind = pltpu.roll(values, HEAD_DIM // 2, 1)
    return values * cosine + ahead * sine_first + behind * sine_second


def lower_mask():
    return row_ids((SPAN, SPAN)) >= lane_ids((SPAN, SPAN))


def span_sums(values):
    lower = jnp.where(lower_mask(), 1.0, 0.0).astype(BF16)
    out = []
    for start in range(0, values.shape[0], SPAN):
        total = None
        for term in pieces(values[start : start + SPAN], 3):
            part = mm(lower, term)
            total = part if total is None else total + part
        out.append(total)
    return jnp.concatenate(out, axis=0)


def span_sums_rows(values):
    upper = jnp.where(row_ids((SPAN, SPAN)) <= lane_ids((SPAN, SPAN)), 1.0, 0.0).astype(BF16)
    out = []
    for start in range(0, values.shape[1], SPAN):
        total = None
        for term in pieces(values[:, start : start + SPAN], 3):
            part = mm(term, upper)
            total = part if total is None else total + part
        out.append(total)
    return jnp.concatenate(out, axis=1)


def span_sums_back(values):
    upper = jnp.where(row_ids((SPAN, SPAN)) <= lane_ids((SPAN, SPAN)), 1.0, 0.0).astype(BF16)
    out = []
    for start in range(0, values.shape[0], SPAN):
        total = None
        for term in pieces(values[start : start + SPAN], 3):
            part = mm(upper, term)
            total = part if total is None else total + part
        out.append(total)
    return jnp.concatenate(out, axis=0)


def steps_of(tp, tp_row, bias, bias_col, rate, rate_col, length):
    seq_len = tp.shape[0]
    valid = jnp.where(row_ids((seq_len, 1)) < length, 1.0, 0.0)
    valid_row = jnp.where(lane_ids((1, seq_len)) < length, 1.0, 0.0)
    dt = softplus(tp + bias) * valid
    dt_row = softplus(tp_row + bias_col) * valid_row
    cum = span_sums(-(dt * rate))
    cum_row = span_sums_rows(-(dt_row * rate_col))
    return valid, dt, cum, cum_row


def spread(values, head):
    return jnp.broadcast_to(values[:, head : head + 1], (values.shape[0], LANES))


def decays(cum_first, cum_second, cum_row, pair, span):
    rows = slice(span * SPAN, (span + 1) * SPAN)
    lower = lower_mask()
    out = []
    for head, column in ((2 * pair, cum_first), (2 * pair + 1, cum_second)):
        differ = column[rows] - cum_row[head : head + 1, rows]
        out.append(jnp.exp(jnp.where(lower, differ, -1e30)))
    return out


def split_heads(values):
    first = lane_ids(values.shape) < HEAD_DIM
    zero = jnp.zeros_like(values)
    return jnp.concatenate([jnp.where(first, values, zero), jnp.where(first, zero, values)], axis=0)


def state_of(in_map, weighted_first, cum_pair_first):
    to_end = jnp.exp(cum_pair_first[SPAN - 1 : SPAN] - cum_pair_first)
    ending = (weighted_first * to_end).astype(BF16)
    return to_end, ending, mm_tn(in_map[:SPAN], ending)


def mixer_forward_kernel(
    len_ref, h_ref, wq_ref, wkv_ref, wz_ref, wx_ref, wb_ref, wc_ref, wt_ref, cxw_ref, cxb_ref,
    cbw_ref, cbb_ref, bias_ref, rate_ref, bias_col_ref, rate_col_ref, skip_ref, cos_ref, sa_ref,
    sb_ref, q_ref, kd_ref, vd_ref, z_ref, x_ref, bcp_ref, bc_ref, tp_ref, tpr_ref, y_ref, ss_ref,
):
    h = h_ref[...]
    pairs = wx_ref.shape[1] // LANES
    z_ref[...] = mm(h, wz_ref[...])
    x_ref[...] = mm(h, wx_ref[...])
    bcp_ref[:, :STATE] = mm(h, wb_ref[...])
    bcp_ref[:, STATE:] = mm(h, wc_ref[...])
    tp = mm_nt(h, wt_ref[...])
    tp_row = mm_nt(wt_ref[...], h)
    tp_ref[...] = tp
    tpr_ref[...] = tp_row
    cosine, sine_first, sine_second = cos_ref[...], sa_ref[...], sb_ref[...]
    for pair in range(wq_ref.shape[1] // LANES):
        lanes = slice(pair * LANES, (pair + 1) * LANES)
        q_ref[:, lanes] = rope(mm(h, wq_ref[:, lanes]), cosine, sine_first, sine_second).astype(BF16)
    kv = mm(h, wkv_ref[...])
    turned = pltpu.roll(kv, HEAD_DIM, 1)
    first = lane_ids(kv.shape) < HEAD_DIM
    kd_ref[...] = rope(jnp.where(first, kv, turned), cosine, sine_first, sine_second).astype(BF16)
    vd_ref[...] = jnp.where(first, turned, kv).astype(BF16)

    mapped = conv(bcp_ref[...], cbw_ref[...], cbb_ref[...])
    bc = (mapped * sigmoid(mapped)).astype(BF16)
    bc_ref[...] = bc
    in_map, out_map = bc[:, :STATE], bc[:, STATE:]
    affinity = [
        mm_nt(out_map[s * SPAN : (s + 1) * SPAN], in_map[s * SPAN : (s + 1) * SPAN]) for s in range(2)
    ]
    _, dt, cum, cum_row = steps_of(
        tp, tp_row, bias_ref[...], bias_col_ref[...], rate_ref[...], rate_col_ref[...], len_ref[0]
    )
    squares = None
    for pair in range(pairs):
        lanes = slice(pair * LANES, (pair + 1) * LANES)
        cx = conv(x_ref[:, lanes], cxw_ref[:, lanes], cxb_ref[:, lanes])
        xc = cx * sigmoid(cx)
        dt_pair = jnp.where(first, spread(dt, 2 * pair), spread(dt, 2 * pair + 1))
        cum_first, cum_second = spread(cum, 2 * pair), spread(cum, 2 * pair + 1)
        cum_pair = jnp.where(first, cum_first, cum_second)
        weighted = xc * dt_pair
        low = weighted.astype(BF16)
        _, _, state = state_of(in_map, weighted[:SPAN], cum_pair[:SPAN])
        parts = []
        for s in range(2):
            rows = slice(s * SPAN, (s + 1) * SPAN)
            mats = [
                (affinity[s] * decay).astype(BF16)
                for decay in decays(cum_first, cum_second, cum_row, pair, s)
            ]
            part = mm(jnp.concatenate(mats, axis=1), split_heads(low[rows]))
            if s:
                part = part + mm(out_map[rows], state.astype(BF16)) * jnp.exp(cum_pair[rows])
            parts.append(part)
        y = jnp.concatenate(parts, axis=0)
        y_ref[:, lanes] = y
        z = z_ref[:, lanes]
        gated = (y + skip_ref[:, lanes] * xc) * (z * sigmoid(z))
        square = gated * gated
        squares = square if squares is None else squares + square
    ss_ref[...] = row_sums(squares)


def masked_probs(queries, kd, length, scale):
    seq_len = kd.shape[0]
    scores = mm_nt(split_heads(queries), kd) * scale
    rows = row_ids(scores.shape)
    rows = jnp.where(rows >= seq_len, rows - seq_len, rows)
    columns = lane_ids(scores.shape)
    scores = jnp.where((rows >= columns) & (columns < length), scores, -1e30)
    weights = jnp.exp(scores - jnp.max(scores, axis=1, keepdims=True))
    return weights / jnp.sum(weights, axis=1, keepdims=True)


def attend_kernel(len_ref, q_ref, kd_ref, vd_ref, out_ref):
    seq_len = q_ref.shape[0]
    values = split_heads(vd_ref[...])
    for pair in range(q_ref.shape[1] // LANES):
        lanes = slice(pair * LANES, (pair + 1) * LANES)
        probs = masked_probs(q_ref[:, lanes], kd_ref[...], len_ref[0], HEAD_DIM ** (-0.5)).astype(BF16)
        both = jnp.concatenate([probs[:seq_len], probs[seq_len:]], axis=1)
        out_ref[:, lanes] = mm(both, values).astype(BF16)


def join_halves(values):
    return values + pltpu.roll(values, HEAD_DIM, 1)


def attend_back_kernel(len_ref, q_ref, kd_ref, vd_ref, da_ref, cos_ref, sa_ref, sb_ref, dq_ref, dkv_ref):
    seq_len = q_ref.shape[0]
    scale = HEAD_DIM ** (-0.5)
    cosine, sine_first, sine_second = cos_ref[...], -sa_ref[...], -sb_ref[...]
    kd, vd = kd_ref[...], vd_ref[...]
    keys = split_heads(kd)
    grad_k, grad_v = None, None
    for pair in range(q_ref.shape[1] // LANES):
        lanes = slice(pair * LANES, (pair + 1) * LANES)
        probs = masked_probs(q_ref[:, lanes], kd, len_ref[0], scale)
        da = split_heads(da_ref[:, lanes])
        dprob = mm_nt(da, vd)
        dscore = (probs * (dprob - jnp.sum(probs * dprob, axis=1, keepdims=True))).astype(BF16)
        both = jnp.concatenate([dscore[:seq_len], dscore[seq_len:]], axis=1)
        dq = mm(both, keys) * scale
        dq_ref[:, lanes] = rope(dq, cosine, sine_first, sine_second).astype(BF16)
        part_k = mm_tn(dscore, split_heads(q_ref[:, lanes]))
        part_v = mm_tn(probs.astype(BF16), da)
        grad_k = part_k if grad_k is None else grad_k + part_k
        grad_v = part_v if grad_v is None else grad_v + part_v
    dk = rope(join_halves(grad_k) * scale, cosine, sine_first, sine_second)
    first = lane_ids(dk.shape) < HEAD_DIM
    dkv_ref[...] = jnp.where(first, dk, join_halves(grad_v)).astype(BF16)


def out_kernel(att_ref, y_ref, x_ref, z_ref, ss_ref, cxw_ref, cxb_ref, skip_ref, gain_ref, wa_ref, ws_ref,
               part_ref, mix_ref, *, width):
    total = mm(att_ref[...], wa_ref[...])
    inv = column_of(lax.rsqrt(ss_ref[...] / width + EPSILON))
    for pair in range(y_ref.shape[1] // LANES):
        lanes = slice(pair * LANES, (pair + 1) * LANES)
        cx = conv(x_ref[:, lanes], cxw_ref[:, lanes], cxb_ref[:, lanes])
        z = z_ref[:, lanes]
        gated = (y_ref[:, lanes] + skip_ref[:, lanes] * (cx * sigmoid(cx))) * (z * sigmoid(z))
        mix_ref[:, lanes] = (gated * inv * gain_ref[:, lanes]).astype(BF16)
    part_ref[...] = (total + mm(mix_ref[...], ws_ref[...])).astype(part_ref.dtype)


def mix_grad_kernel(db_ref, y_ref, x_ref, z_ref, cxw_ref, cxb_ref, skip_ref, gain_ref, wa_ref, ws_ref,
                    da_ref, dm_ref, bs_ref):
    db = db_ref[...]
    da_ref[...] = mm_nt(db, wa_ref[...]).astype(BF16)
    dm_ref[...] = mm_nt(db, ws_ref[...]).astype(BF16)
    total = None
    for pair in range(y_ref.shape[1] // LANES):
        lanes = slice(pair * LANES, (pair + 1) * LANES)
        cx = conv(x_ref[:, lanes], cxw_ref[:, lanes], cxb_ref[:, lanes])
        z = z_ref[:, lanes]
        gated = (y_ref[:, lanes] + skip_ref[:, lanes] * (cx * sigmoid(cx))) * (z * sigmoid(z))
        part = gated * (gain_ref[:, lanes] * dm_ref[:, lanes].astype(F32))
        total = part if total is None else total + part
    bs_ref[...] = row_sums(total)


def head_sums(values, pair):
    rows, columns = row_ids((LANES, 16)), lane_ids((LANES, 16))
    chosen = jnp.where(columns == 2 * pair + jnp.where(rows < HEAD_DIM, 0, 1), 1.0, 0.0).astype(BF16)
    high, low = pieces(values, 2)
    return mm(jnp.concatenate([high, low], axis=1), jnp.concatenate([chosen, chosen], axis=0))


def mixer_back_kernel(
    len_ref, dm_ref, y_ref, x_ref, z_ref, bcp_ref, bc_ref, tp_ref, tpr_ref, ss_ref, bs_ref, dq_ref,
    dkv_ref, wq_ref, wkv_ref, wz_ref, wx_ref, wb_ref, wc_ref, wt_ref, cxw_ref, cxb_ref, cbw_ref,
    cbb_ref, bias_ref, rate_ref, bias_col_ref, rate_col_ref, skip_ref, gain_ref,
    dh_ref, dx_ref, dz_ref, dbc_ref, dt_ref, wide_ref, bcg_ref, small_ref, *, width,
):
    pairs = x_ref.shape[1] // LANES
    bc = bc_ref[...]
    in_map, out_map = bc[:, :STATE], bc[:, STATE:]
    affinity = [
        mm_nt(out_map[s * SPAN : (s + 1) * SPAN], in_map[s * SPAN : (s + 1) * SPAN]) for s in range(2)
    ]
    valid, dt, cum, cum_row = steps_of(
        tp_ref[...], tpr_ref[...], bias_ref[...], bias_col_ref[...], rate_ref[...], rate_col_ref[...], len_ref[0]
    )
    inv_row = lax.rsqrt(ss_ref[...] / width + EPSILON)
    inv = column_of(inv_row)
    back = column_of(inv_row * inv_row * inv_row * bs_ref[...] / width)
    first = lane_ids((x_ref.shape[0], LANES)) < HEAD_DIM
    last_row = row_ids((SPAN, LANES)) == SPAN - 1
    d_cum, d_step = None, None
    d_aff, d_out, d_in = [None, None], None, None

    def plus(total, part):
        return part if total is None else total + part

    for pair in range(pairs):
        lanes = slice(pair * LANES, (pair + 1) * LANES)
        x = x_ref[:, lanes]
        cxw = cxw_ref[:, lanes]
        cx = conv(x, cxw, cxb_ref[:, lanes])
        sx = sigmoid(cx)
        xc = cx * sx
        z = z_ref[:, lanes]
        sz = sigmoid(z)
        silu_z = z * sz
        scanned = y_ref[:, lanes]
        y = scanned + skip_ref[:, lanes] * xc
        gated = y * silu_z
        d_mix = dm_ref[:, lanes].astype(F32)
        d_gated = inv * (gain_ref[:, lanes] * d_mix) - gated * back
        wide_ref[6:7, lanes] = jnp.sum(d_mix * gated * inv, axis=0, keepdims=True)
        dy = d_gated * silu_z
        dz_ref[:, lanes] = (d_gated * y * (sz * (1.0 + z * (1.0 - sz)))).astype(BF16)
        wide_ref[5:6, lanes] = jnp.sum(dy * xc, axis=0, keepdims=True)
        dt_pair = jnp.where(first, spread(dt, 2 * pair), spread(dt, 2 * pair + 1))
        cum_first, cum_second = spread(cum, 2 * pair), spread(cum, 2 * pair + 1)
        cum_pair = jnp.where(first, cum_first, cum_second)
        weighted = xc * dt_pair
        low = weighted.astype(BF16)
        dy_low = dy.astype(BF16)
        to_end, ending, state = state_of(in_map, weighted[:SPAN], cum_pair[:SPAN])
        d_weighted = []
        for s in range(2):
            rows = slice(s * SPAN, (s + 1) * SPAN)
            decay = decays(cum_first, cum_second, cum_row, pair, s)
            mats = jnp.concatenate([(affinity[s] * one).astype(BF16) for one in decay], axis=0)
            both = split_heads(dy_low[rows])
            d_mats = mm_nt(both, low[rows])
            d_aff[s] = plus(d_aff[s], d_mats[:SPAN] * decay[0] + d_mats[SPAN:] * decay[1])
            d_weighted.append(mm_tn(mats, both))
        reached = (dy[SPAN:] * jnp.exp(cum_pair[SPAN:])).astype(BF16)
        d_out = plus(d_out, mm_nt(reached, state.astype(BF16)))
        d_state = mm_tn(out_map[SPAN:], reached).astype(BF16)
        d_in = plus(d_in, mm_nt(ending, d_state))
        d_ending = mm(in_map[:SPAN], d_state)
        through = ending.astype(F32) * d_ending
        low_f, dy_f = low.astype(F32), dy_low.astype(F32)
        change = dy_f * scanned - low_f * jnp.concatenate(d_weighted, axis=0)
        ended = jnp.where(last_row, jnp.sum(through, axis=0, keepdims=True), 0.0) - through
        change = jnp.concatenate([change[:SPAN] + ended, change[SPAN:]], axis=0)
        d_weight = jnp.concatenate([d_weighted[0] + d_ending * to_end, d_weighted[1]], axis=0)
        d_cum = plus(d_cum, head_sums(change, pair))
        d_step = plus(d_step, head_sums(d_weight * xc, pair))
        d_xc = dy * skip_ref[:, lanes] + d_weight * dt_pair
        d_cx = d_xc * (sx * (1.0 + cx * (1.0 - sx)))
        d_x, rows_x = conv_back(d_cx, x, cxw)
        dx_ref[:, lanes] = d_x.astype(BF16)
        for index, row in enumerate(rows_x):
            wide_ref[index : index + 1, lanes] = row

    rate = rate_ref[...]
    d_log = span_sums_back(d_cum)
    d_dt = d_step - rate * d_log
    d_tp = d_dt * valid * sigmoid(tp_ref[...] + bias_ref[...])
    small_ref[...] = jnp.zeros(small_ref.shape, F32)
    small_ref[0:1, :] = jnp.sum(d_tp, axis=0, keepdims=True)
    small_ref[1:2, :] = -rate * jnp.sum(dt * d_log, axis=0, keepdims=True)
    dt_ref[...] = d_tp.astype(BF16)

    d_maps = []
    low_aff = [part.astype(BF16) for part in d_aff]
    d_ins, d_outs = [], []
    for s in range(2):
        rows = slice(s * SPAN, (s + 1) * SPAN)
        d_outs.append(mm(low_aff[s], in_map[rows]))
        d_ins.append(mm_tn(low_aff[s], out_map[rows]))
    d_outs[1] = d_outs[1] + d_out
    d_ins[0] = d_ins[0] + d_in
    d_maps = jnp.concatenate(
        [jnp.concatenate(d_ins, axis=0), jnp.concatenate(d_outs, axis=0)], axis=1
    )
    mapped = conv(bcp_ref[...], cbw_ref[...], cbb_ref[...])
    sm = sigmoid(mapped)
    d_bc, rows_bc = conv_back(d_maps * (sm * (1.0 + mapped * (1.0 - sm))), bcp_ref[...], cbw_ref[...])
    bcg_ref[...] = jnp.zeros(bcg_ref.shape, F32)
    for index, row in enumerate(rows_bc):
        bcg_ref[index : index + 1, :] = row
    d_bc = d_bc.astype(BF16)
    dbc_ref[...] = d_bc
    total = mm_nt(dx_ref[...], wx_ref[...]) + mm_nt(dz_ref[...], wz_ref[...])
    total = total + mm_nt(dq_ref[...], wq_ref[...]) + mm_nt(dkv_ref[...], wkv_ref[...])
    total = total + mm_nt(d_bc[:, :STATE], wb_ref[...]) + mm_nt(d_bc[:, STATE:], wc_ref[...])
    total = total + mm(dt_ref[...], wt_ref[...])
    dh_ref[...] = total.astype(dh_ref.dtype)


def ffn_kernel(h_ref, ct_ref, wg_ref, wu_ref, wd_ref, hid_ref, dg_ref, du_ref, ff_ref, dh_ref, ff_acc, dh_acc):
    step = pl.program_id(0)
    h = h_ref[...]
    gate = mm(h, wg_ref[...])
    up = mm(h, wu_ref[...])
    d_hidden = mm_nt(ct_ref[...], wd_ref[...]).astype(BF16).astype(F32)
    sg = sigmoid(gate)
    silu = gate * sg
    hidden = (silu * up).astype(BF16)
    d_gate = (d_hidden * up * (sg * (1.0 + gate * (1.0 - sg)))).astype(BF16)
    d_up = (d_hidden * silu).astype(BF16)
    hid_ref[...] = hidden
    dg_ref[...] = d_gate
    du_ref[...] = d_up
    ff_part = mm(hidden, wd_ref[...])
    dh_part = mm_nt(d_gate, wg_ref[...]) + mm_nt(d_up, wu_ref[...])

    @pl.when(step == 0)
    def _():
        ff_acc[...] = ff_part
        dh_acc[...] = dh_part

    @pl.when(step > 0)
    def _():
        ff_acc[...] += ff_part
        dh_acc[...] += dh_part

    @pl.when(step == pl.num_programs(0) - 1)
    def _():
        ff_ref[...] = ff_acc[...].astype(ff_ref.dtype)
        dh_ref[...] = dh_acc[...].astype(dh_ref.dtype)


def shaped(shape, dtype=F32):
    return jax.ShapeDtypeStruct(shape, dtype)


def whole_call(kernel, outs, scalars, args, flops, name):
    specs = [pl.BlockSpec(memory_space=pltpu.SMEM)] * scalars
    specs += [pl.BlockSpec(memory_space=pltpu.VMEM)] * (len(args) - scalars)
    moved = sum(arg.size * arg.dtype.itemsize for arg in args)
    return pl.pallas_call(
        kernel,
        out_shape=outs,
        in_specs=specs,
        out_specs=[pl.BlockSpec(memory_space=pltpu.VMEM)] * len(outs),
        compiler_params=pltpu.CompilerParams(vmem_limit_bytes=VMEM_LIMIT),
        cost_estimate=pl.CostEstimate(flops=flops, bytes_accessed=moved, transcendentals=0),
        name=name,
    )(*args)


def pad_columns(values, width):
    return jnp.pad(values, ((0, 0), (0, width - values.shape[1]))) if width != values.shape[1] else values


def pad_rows(values, height):
    return jnp.pad(values, ((0, height - values.shape[0]), (0, 0))) if height != values.shape[0] else values


def contract_rows(left, right):
    return mm_tn(jnp.concatenate(left, axis=0), jnp.concatenate(right, axis=0))


def on_device(
    tokens, lengths, cotangent, norm_gain, w_query, w_key, w_value, w_gate_z, w_ssm_x, w_ssm_b, w_ssm_c,
    w_step, conv_x_weight, conv_x_bias, conv_bc_weight, conv_bc_bias, step_bias, decay_log, skip_gain,
    ssm_norm_gain, w_out_att, w_out_ssm, ffn_norm_gain, w_gate, w_up, w_down,
):
    seq_len, model = tokens.shape
    groups = lax.axis_size("tensor")
    position = lax.axis_index("tensor")
    att_width, ssm_width = w_query.shape[1], w_gate_z.shape[1]
    att_pad = -(-att_width // LANES) * LANES
    ssm_pad = -(-ssm_width // LANES) * LANES
    ssm_heads = ssm_width // SSM_DIM
    ssm_width_all = SSM_HEADS * SSM_DIM
    ff_width = w_gate.shape[1]

    def fetch(values, shift):
        return lax.ppermute(values, "tensor", [((i + shift) % groups, i) for i in range(groups)])

    def deliver(values, shift):
        return lax.ppermute(values, "tensor", [(i, (i + shift) % groups) for i in range(groups)])

    def gather(values):
        return [values] + [fetch(values, k) for k in range(1, groups)]

    def scatter_sum(own, others):
        total = own
        for k in range(1, groups):
            total = total + deliver(others[k - 1], k).astype(F32)
        return total

    kv_head = position * (att_width // HEAD_DIM) // (HEADS // KV_HEADS)
    w_kv = jnp.concatenate(
        [lax.dynamic_slice_in_dim(w, kv_head * HEAD_DIM, HEAD_DIM, 1) for w in (w_key, w_value)], axis=1
    )
    wq = pad_columns(w_query, att_pad)
    wz, wx = pad_columns(w_gate_z, ssm_pad), pad_columns(w_ssm_x, ssm_pad)
    wt = pad_rows(w_step.T, 16)
    wa, ws = pad_rows(w_out_att, att_pad), pad_rows(w_out_ssm, ssm_pad)
    cxw, cxb = pad_columns(conv_x_weight, ssm_pad), pad_columns(conv_x_bias[None], ssm_pad)
    cbb = conv_bc_bias[None]
    gain = pad_columns(ssm_norm_gain[None], ssm_pad)
    skip = pad_columns(jnp.repeat(skip_gain, SSM_DIM)[None], ssm_pad)
    bias = pad_columns(step_bias[None], 16)
    rate = pad_columns(jnp.exp(decay_log)[None], 16)
    bias_col, rate_col = bias.T, rate.T
    half = HEAD_DIM // 2
    freqs = ROPE_BASE ** (-(jnp.arange(half).astype(F32) * 2.0 / HEAD_DIM))
    angles = jnp.arange(seq_len).astype(F32)[:, None] * freqs[None, :]
    cosine, sine, none = jnp.cos(angles), jnp.sin(angles), jnp.zeros_like(angles)
    cos_table = jnp.concatenate([cosine] * 4, axis=1)
    sine_first = jnp.concatenate([-sine, none] * 2, axis=1)
    sine_second = jnp.concatenate([none, sine] * 2, axis=1)

    inputs = tokens.astype(F32)
    inv1 = lax.rsqrt(jnp.mean(inputs * inputs, axis=1, keepdims=True) + EPSILON)
    h_own = (inputs * inv1 * norm_gain).astype(BF16)
    own_mask = jnp.arange(seq_len) < lengths[0]
    ct_own = jnp.where(own_mask[:, None], cotangent, jnp.zeros_like(cotangent))
    h_all = gather(h_own)
    len_all = gather(lengths)
    ct_all = gather(ct_own)

    def forward(k):
        outs = [
            shaped((seq_len, att_pad), BF16), shaped((seq_len, LANES), BF16), shaped((seq_len, LANES), BF16),
            shaped((seq_len, ssm_pad)), shaped((seq_len, ssm_pad)), shaped((seq_len, 2 * STATE)),
            shaped((seq_len, 2 * STATE), BF16), shaped((seq_len, 16)), shaped((16, seq_len)),
            shaped((seq_len, ssm_pad)), shaped((16, seq_len)),
        ]
        args = [
            len_all[k], h_all[k], wq, w_kv, wz, wx, w_ssm_b, w_ssm_c, wt, cxw, cxb, conv_bc_weight, cbb,
            bias, rate, bias_col, rate_col, skip, cos_table, sine_first, sine_second,
        ]
        return whole_call(mixer_forward_kernel, outs, 1, args, 8 * 10**9, "mixer_forward")

    def attend(k):
        q, kd, vd = kept[k][:3]
        return whole_call(
            attend_kernel, [shaped((seq_len, att_pad), BF16)], 1, [len_all[k], q, kd, vd], 2 * 10**9, "attend"
        )[0]

    kept = [forward(k) for k in range(groups)]
    squares_part = [one[10] for one in kept]
    squares = [squares_part[k] for k in range(groups)]
    for shift in range(1, groups):
        for k in range(groups):
            squares[k] = squares[k] + fetch(squares_part[(k - shift) % groups], shift)
    mix_att = [attend(k) for k in range(groups)]

    def project(k, dtype):
        q, kd, vd, z, x, bcp, bc, tp, tpr, y, _ = kept[k]
        return whole_call(
            functools.partial(out_kernel, width=ssm_width_all),
            [shaped((seq_len, model), dtype), shaped((seq_len, ssm_pad), BF16)],
            0,
            [mix_att[k], y, x, z, squares[k], cxw, cxb, skip, gain, wa, ws],
            4 * 10**9,
            "out_project",
        )

    projected = [project(k, F32 if k == 0 else BF16) for k in range(groups)]
    mix_ssm = [one[1] for one in projected]
    branch = scatter_sum(projected[0][0], [one[0] for one in projected[1:]])
    resid = inputs + branch
    inv2 = lax.rsqrt(jnp.mean(resid * resid, axis=1, keepdims=True) + EPSILON)
    h2_own = (resid * inv2 * ffn_norm_gain).astype(BF16)
    h2_all = gather(h2_own)

    def feed(k):
        dtype = F32 if k == 0 else BF16
        block = min(256, ff_width)
        full = pl.BlockSpec((seq_len, model), lambda i: (0, 0))
        columns = pl.BlockSpec((model, block), lambda i: (0, i))
        rows = pl.BlockSpec((block, model), lambda i: (i, 0))
        tall = pl.BlockSpec((seq_len, block), lambda i: (0, i))
        return pl.pallas_call(
            ffn_kernel,
            grid=(ff_width // block,),
            out_shape=[shaped((seq_len, ff_width), BF16)] * 3 + [shaped((seq_len, model), dtype)] * 2,
            in_specs=[full, full, columns, columns, rows],
            out_specs=[tall] * 3 + [full] * 2,
            scratch_shapes=[pltpu.VMEM((seq_len, model), F32)] * 2,
            compiler_params=pltpu.CompilerParams(vmem_limit_bytes=VMEM_LIMIT),
            cost_estimate=pl.CostEstimate(flops=8 * 10**9, bytes_accessed=10**7, transcendentals=0),
            name="feed_forward",
        )(h2_all[k], ct_all[k], w_gate, w_up, w_down)

    fed = [feed(k) for k in range(groups)]
    d_second = scatter_sum(fed[0][4], [one[4] for one in fed[1:]])
    ffn_result = scatter_sum(fed[0][3], [one[3] for one in fed[1:]])
    layer_output = (resid + ffn_result).astype(BF16)
    grad_gate = contract_rows(h2_all, [one[1] for one in fed])
    grad_up = contract_rows(h2_all, [one[2] for one in fed])
    grad_down = contract_rows([one[0] for one in fed], ct_all)

    scaled = d_second * ffn_norm_gain
    d_resid = (
        ct_own.astype(F32)
        + inv2 * scaled
        - resid * (inv2**3) * jnp.mean(scaled * resid, axis=1, keepdims=True)
    )
    grad_ffn_gain = jnp.sum(d_second * resid * inv2, axis=0)
    db_all = gather(d_resid.astype(BF16))

    def mix_grad(k):
        q, kd, vd, z, x, bcp, bc, tp, tpr, y, _ = kept[k]
        return whole_call(
            mix_grad_kernel,
            [shaped((seq_len, att_pad), BF16), shaped((seq_len, ssm_pad), BF16), shaped((16, seq_len))],
            0,
            [db_all[k], y, x, z, cxw, cxb, skip, gain, wa, ws],
            4 * 10**9,
            "mix_grad",
        )

    mixed = [mix_grad(k) for k in range(groups)]
    backs_part = [one[2] for one in mixed]
    backs = [backs_part[k] for k in range(groups)]
    for shift in range(1, groups):
        for k in range(groups):
            backs[k] = backs[k] + fetch(backs_part[(k - shift) % groups], shift)

    def attend_back(k):
        q, kd, vd = kept[k][:3]
        return whole_call(
            attend_back_kernel,
            [shaped((seq_len, att_pad), BF16), shaped((seq_len, LANES), BF16)],
            1,
            [len_all[k], q, kd, vd, mixed[k][0], cos_table, sine_first, sine_second],
            4 * 10**9,
            "attend_back",
        )

    turned = [attend_back(k) for k in range(groups)]

    def backward(k):
        q, kd, vd, z, x, bcp, bc, tp, tpr, y, _ = kept[k]
        outs = [
            shaped((seq_len, model), F32 if k == 0 else BF16), shaped((seq_len, ssm_pad), BF16),
            shaped((seq_len, ssm_pad), BF16), shaped((seq_len, 2 * STATE), BF16), shaped((seq_len, 16), BF16),
            shaped((8, ssm_pad)), shaped((8, 2 * STATE)), shaped((8, 16)),
        ]
        args = [
            len_all[k], mixed[k][1], y, x, z, bcp, bc, tp, tpr, squares[k], backs[k], turned[k][0], turned[k][1],
            wq, w_kv, wz, wx, w_ssm_b, w_ssm_c, wt, cxw, cxb, conv_bc_weight, cbb, bias, rate, bias_col, rate_col,
            skip, gain,
        ]
        return whole_call(
            functools.partial(mixer_back_kernel, width=ssm_width_all), outs, 1, args, 16 * 10**9, "mixer_back"
        )

    gone = [None] * groups
    for k in list(range(1, groups)) + [0]:
        gone[k] = backward(k)
    d_first = scatter_sum(gone[0][0], [one[0] for one in gone[1:]])
    scaled = d_first * norm_gain
    grad_input = (
        d_resid
        + inv1 * scaled
        - inputs * (inv1**3) * jnp.mean(scaled * inputs, axis=1, keepdims=True)
    )
    grad_norm_gain = jnp.sum(d_first * inputs * inv1, axis=0)

    grad_out_att = contract_rows(mix_att, db_all)[:att_width]
    grad_out_ssm = contract_rows(mix_ssm, db_all)[:ssm_width]
    grad_query = contract_rows(h_all, [one[0] for one in turned])[:, :att_width]
    grad_kv = contract_rows(h_all, [one[1] for one in turned])
    grad_x = contract_rows(h_all, [one[1] for one in gone])[:, :ssm_width]
    grad_z = contract_rows(h_all, [one[2] for one in gone])[:, :ssm_width]
    grad_bc = contract_rows(h_all, [one[3] for one in gone])
    grad_step = contract_rows(h_all, [one[4] for one in gone])[:, :ssm_heads]
    wide, bcg, small = (sum(one[i] for one in gone) for i in (5, 6, 7))
    grad_skip = jnp.sum(wide[5, :ssm_width].reshape(ssm_heads, SSM_DIM), axis=1)

    def total_dp(values):
        return lax.psum(values.astype(BF16), "dp").astype(F32)

    zeros = jnp.zeros((model, KV_HEADS * HEAD_DIM), F32)
    grad_key = lax.dynamic_update_slice(zeros, grad_kv[:, :HEAD_DIM], (0, kv_head * HEAD_DIM))
    grad_value = lax.dynamic_update_slice(zeros, grad_kv[:, HEAD_DIM:], (0, kv_head * HEAD_DIM))
    grad_key, grad_value, grad_bc, bcg, grad_norm_gain, grad_ffn_gain = lax.psum(
        (grad_key, grad_value, grad_bc, bcg, grad_norm_gain, grad_ffn_gain), ("dp", "tensor")
    )
    return (
        layer_output,
        grad_input,
        grad_norm_gain,
        total_dp(grad_query),
        grad_key,
        grad_value,
        total_dp(grad_z),
        total_dp(grad_x),
        grad_bc[:, :STATE],
        grad_bc[:, STATE:],
        total_dp(grad_step),
        total_dp(wide[:4, :ssm_width]),
        total_dp(wide[4, :ssm_width]),
        bcg[:4],
        bcg[4],
        total_dp(small[0, :ssm_heads]),
        total_dp(small[1, :ssm_heads]),
        total_dp(grad_skip),
        total_dp(wide[6, :ssm_width]),
        total_dp(grad_out_att),
        total_dp(grad_out_ssm),
        grad_ffn_gain,
        total_dp(grad_gate),
        total_dp(grad_up),
        total_dp(grad_down),
    )


def solution(mesh):
    rows, split, tall = P(("dp", "tensor"), None), P(None, "tensor"), P("tensor", None)
    vector, copied = P("tensor"), P()
    return jax.shard_map(
        on_device,
        mesh=mesh,
        in_specs=(
            rows, P(("dp", "tensor")), rows, copied, split, copied, copied, split, split, copied, copied, split,
            split, vector, copied, copied, vector, vector, vector, vector, tall, tall, copied, split, split, tall,
        ),
        out_specs=(
            rows, rows, copied, split, copied, copied, split, split, copied, copied, split, split, vector, copied,
            copied, vector, vector, vector, vector, tall, tall, copied, split, split, tall,
        ),
        check_vma=False,
    )
```

time: 849 us -> 589 us (0.69)
  waiting for transfers between devices: 393 us -> 280 us
  matrix products: 133 us -> 21.4 us
  Pallas kernels: 0 us -> 82.8 us
  local copies, waits for them, and re-layouts: 93.1 us -> 35.8 us
  other arithmetic: 89.6 us -> 37.1 us
  blocking collectives: 117 us -> 95.1 us
  starting transfers between devices: 0.67 us -> 14.8 us
    dot_general x68 -> x11, matrix products: 133 us -> 21.4 us  [mm_tn(): lax.dot_general(left, right, (((0,), (0,)), ((), ())), preferred_element_...]
    pallas_call x0 -> x14, Pallas kernels: none -> 82.8 us  [the longest x12 67.5 us: whole_call(): pl.pallas_call(kernel, out_shape=outs, in_specs=specs, out_specs=[pl.Bloc...]
    reduce_scatter x5 -> x0, waiting for transfers between devices: 75.2 us -> none  [the longest x1 29.3 us: on_device(): lax.psum_scatter(jnp.dot(mix_att, w_out_att, preferred_element_type=jnp.f...]
    all_gather x4 -> x0, waiting for transfers between devices: 65.9 us -> none  [the longest x1 19.2 us: on_device(): second_all = lax.all_gather(second_normed, 'tensor', axis=0, tiled=True)]
    ppermute x0 -> x13, waiting for transfers between devices: none -> 31.6 us  [the longest x9 24.8 us: fetch(): lax.ppermute(values, 'tensor', [((i + shift) % groups, i) for i in range(...]
    reshape x16 -> x0, local copies, waits for them, and re-layouts: 28.4 us -> none  [the longest x3 9.71 us: ssd_scan(): return (inner_part + outer_part).reshape(seq_steps, num_heads, head_width)]
    reduce_sum x16 -> x5, other arithmetic: 23.2 us -> 6.11 us  [the longest x1 1.66 us: on_device(): inv2 = lax.rsqrt(jnp.mean(resid * resid, axis=1, keepdims=True) + EPSILON)]
    psum x4 -> x2, blocking collectives: 112 us -> 95.1 us  [the longest x1 57.8 us: total_dp(): return lax.psum(values.astype(BF16), 'dp').astype(F32)]
  transfers between devices with their start and end apart: 11 -> 15, of which waited for: 9 -> 6; matrix products, arithmetic and copies ran while one was open for 11% -> 9% of each run, Pallas kernels for 0% -> 11%
where the time goes in v1:
time: 589 us; the launch traced here: 583 us
  waiting for transfers between devices  280 us (48%)
  blocking collectives  95.1 us (16%)
  Pallas kernels  82.8 us (14%)
  other arithmetic  37.1 us (6%)
  local copies, waits for them, and re-layouts  35.8 us (6%)
  matrix products  21.4 us (4%)
  between operations  15.8 us (3%)
  starting transfers between devices  14.8 us (3%)
    psum x1, waiting for transfers between devices, total_dp(): return lax.psum(values.astype(BF16), 'dp').astype(F32)  236 us
    pallas_call x12, Pallas kernels, whole_call(): pl.pallas_call(kernel, out_shape=outs, in_specs=specs, out_specs=[pl.Bloc...  67.5 us
    psum x1, blocking collectives, total_dp(): return lax.psum(values.astype(BF16), 'dp').astype(F32)  57.8 us
    psum x1, blocking collectives, on_device(): lax.psum((grad_key, grad_value, grad_bc, bcg, grad_norm_gain, grad_ffn_ga...  37.2 us
    ppermute x9, waiting for transfers between devices, fetch(): lax.ppermute(values, 'tensor', [((i + shift) % groups, i) for i in range(...  24.8 us
    convert_element_type x15, other arithmetic, total_dp(): return lax.psum(values.astype(BF16), 'dp').astype(F32)  21.6 us
    dot_general x11, matrix products, mm_tn(): lax.dot_general(left, right, (((0,), (0,)), ((), ())), preferred_element_...  21.4 us
    unnamed x174, local copies, waits for them, and re-layouts  18.2 us
  transfers between devices with their start and end apart: 15, of which 6 were waited for; matrix products, arithmetic and copies ran while one was open for 9% of the time, Pallas kernels for 11%

profile of v1, /device:TPU:0, one launch (start us, length us, event | category | flops | bytes accessed | tf_op | source)
XLA Modules:
  0.0 582.7 jit_solution(8928435371901421300)
XLA Ops:
  7.3 3.0 collective-permute-start
  19.7 6.5 %mixer_forward.2 = (bf16[256,256]{1,0:T(8,128)(2,1)S(1)}, bf16[256,128]{1,0:T(8,128)(2,1)S(1)}, bf16[256,128]{1,0:T(8,128)(2,1)S(1)}, f32[256,768]{1,0:T(8,128)S...) custom-call(s32[1]{0:T(128)} %copy.87.len_ref, ...), custom_call_target="tpu_custom_call" | custom-call | flops 8000000000 | bytes 5430532 | tf_op jit(solution)/shard_map/mixer_forward/pallas_call | solution.py:511
  27.6 9.5 %collective-permute-done.1.h_ref = bf16[256,1024]{1,0:T(8,128)(2,1)S(1)} collective-permute-done((bf16[256,1024]{1,0:T(8,128)(2,1)S(1)}, bf16[256,1024]{1,0:T(8,128)(2,1)S(1)}, u32[]{:S(2)}, u32[]{:S(2)}) %collective-permute-start.1) | collective-permute-done | bytes 524320 | tf_op jit(solution)/shard_map/ppermute | solution.py:550
  37.0 7.1 %mixer_forward.3 = (bf16[256,256]{1,0:T(8,128)(2,1)S(1)}, bf16[256,128]{1,0:T(8,128)(2,1)S(1)}, bf16[256,128]{1,0:T(8,128)(2,1)S(1)}, f32[256,768]{1,0:T(8,128)S...) custom-call(s32[1]{0:T(128)} %collective-permute-done.len_ref, ...), custom_call_target="tpu_custom_call" | custom-call | flops 8000000000 | bytes 5430532 | tf_op jit(solution)/shard_map/mixer_forward/pallas_call | solution.py:511
  47.9 3.2 out_project.3
  52.9 13.2 %attend.2.att_ref = bf16[256,256]{1,0:T(8,128)(2,1)S(1)} custom-call(s32[1]{0:T(128)} %copy.87.len_ref, bf16[256,256]{1,0:T(8,128)(2,1)S(1)} %get-tuple-element.87.q_ref, bf16[256,128]{1,0:T(8,128)(2,1)S(1)} %get-tuple-element.88.kd_ref, bf16[256,128]{1,0:T(8,128)(2,1)S(1)} %get-tuple-element.89.vd_ref), custom_call_target="tpu_custom_call" | custom-call | flops 2000000000 | bytes 262148 | tf_op jit(solution)/shard_map/attend/pallas_call | solution.py:511
  66.2 4.2 out_project.2
  73.6 11.5 %collective-permute-done.5.h_ref = bf16[256,1024]{1,0:T(8,128)(2,1)S(1)} collective-permute-done((bf16[256,1024]{1,0:T(8,128)(2,1)S(1)}, bf16[256,1024]{1,0:T(8,128)(2,1)S(1)}, u32[]{:S(2)}, u32[]{:S(2)}) %collective-permute-start.5) | collective-permute-done | bytes 524320 | tf_op jit(solution)/shard_map/ppermute | solution.py:550
  85.0 7.4 %feed_forward.3 = (bf16[256,1024]{1,0:T(8,128)(2,1)S(1)}, bf16[256,1024]{1,0:T(8,128)(2,1)S(1)}, bf16[256,1024]{1,0:T(8,128)(2,1)S(1)}, bf16[256,1024]{1,0:T(8,128)(2,1)S(1)}, bf16[256,1024]{1,0:T(8,128)(2,1)S(1)}) custom-call(bf16[256,1024]{1,0:T(8,128)(2,1)S(1)} %collective-permute-done.5.h_ref, bf16[256,1024]{1,0:T(8,128)(2,1)} %collective-permute-done.6.ct_ref, ...), custom_call_target="tpu_custom_call" | custom-call | flops 8000000000 | bytes 10000000 | tf_op jit(solution)/shard_map/feed_forward/pallas_call | solution.py:649
  94.7 7.9 %feed_forward.2 = (bf16[256,1024]{1,0:T(8,128)(2,1)S(1)}, bf16[256,1024]{1,0:T(8,128)(2,1)S(1)}, bf16[256,1024]{1,0:T(8,128)(2,1)S(1)}, f32[256,1024]{1,0:T(8,128)S(1)}, f32[256,1024]{1,0:T(8,128)}) custom-call(bf16[256,1024]{1,0:T(8,128)(2,1)S(1)} %multiply_convert_fusion.h_ref, bf16[256,1024]{1,0:T(8,128)(2,1)S(1)} %broadcast_select_fusion.ct_ref, ...), custom_call_target="tpu_custom_call" | custom-call | flops 8000000000 | bytes 10000000 | tf_op jit(solution)/shard_map/feed_forward/pallas_call | solution.py:649
  104.0 3.8 convolution_convert_fusion
  109.3 6.8 %collective-permute-done.7 = bf16[256,1024]{1,0:T(8,128)(2,1)S(1)} collective-permute-done((bf16[256,1024]{1,0:T(8,128)(2,1)S(1)}, bf16[256,1024]{1,0:T(8,128)(2,1)S(1)}, u32[]{:S(2)}, u32[]{:S(2)}) %collective-permute-start.7) | collective-permute-done | bytes 524320 | tf_op jit(solution)/shard_map/ppermute | solution.py:553
  119.8 2.9 mix_grad.2
  126.5 3.9 collective-permute-done.9.db_ref
  130.4 3.1 mix_grad.3
  138.5 10.4 %mixer_back.3 = (bf16[256,1024]{1,0:T(8,128)(2,1)S(1)}, bf16[256,768]{1,0:T(8,128)(2,1)S(1)}, bf16[256,768]{1,0:T(8,128)(2,1)S(1)}, bf16[256,256]{1,0:T(8,128)(2...) custom-call(s32[1]{0:T(128)} %collective-permute-done.len_ref, ...), custom_call_target="tpu_custom_call" | custom-call | flops 16000000000 | bytes 7923972 | tf_op jit(solution)/shard_map/mixer_back/pallas_call | solution.py:511
  156.1 3.0 dynamic_update_slice.7
  159.9 3.0 dynamic_update_slice.6
  168.5 10.2 %mixer_back.2 = (f32[256,1024]{1,0:T(8,128)}, bf16[256,768]{1,0:T(8,128)(2,1)S(1)}, bf16[256,768]{1,0:T(8,128)(2,1)S(1)}, bf16[256,256]{1,0:T(8,128)(2,1)S(1)}, ...) custom-call(s32[1]{0:T(128)} %copy.87.len_ref, ...), custom_call_target="tpu_custom_call" | custom-call | flops 16000000000 | bytes 7923972 | tf_op jit(solution)/shard_map/mixer_back/pallas_call | solution.py:511
  182.0 3.9 convolution_convert_fusion.2
  201.1 57.8 %all-reduce.5 = (bf16[1024,12]{0,1:T(8,128)(2,1)S(1)}, bf16[4,768]{1,0:T(4,128)(2,1)S(1)}, bf16[768]{0:T(1024)(128)(2,1)S(1)}, bf16[12]{0:T(256)(128)(2,1)S(1)},...) all-reduce(bf16[1024,12]{0,1:T(8,128)(2,1)S(1)} %bitcast.22, ...), channel_id=1, replica_groups=mesh['dp'=16,'tensor'=2] {'dp'}, use_global_device_ids=true, to_apply=%region_12.13 | all-reduce | flops 16932 | bytes 67728 | tf_op jit(solution)/shard_map/psum | solution.py:749
  264.5 37.2 %all-reduce.3 = (f32[1024]{0:T(1024)}, f32[8,256]{1,0:T(8,128)S(1)}, f32[1024]{0:T(1024)}) all-reduce(f32[1024]{0:T(1024)S(1)} %get-tuple-element.151, f32[8,256]{1,0:T(8,128)S(1)} %add.138, f32[1024]{0:T(1024)S(1)} %get-tuple-element.149), channel_id=1, replica_groups=mesh['dp'=16,'tensor'=2] {'dp','tensor'}, use_global_device_ids=true, to_apply=%region_5.6 | all-reduce | flops 4096 | bytes 32768 | tf_op jit(solution)/shard_map/psum | solution.py:754
  305.8 11.8 %all-reduce.10.cloned.1.call-done = (f32[1024,128]{1,0:T(8,128)}, f32[1024,128]{1,0:T(8,128)}, f32[1024,256]{1,0:T(8,128)}) async-done(((f32[1024,128]{1,0:T(8,128)}, f32[1024,128]{1,0:T(8,128)}, f32[1024,256]{1,0:T(8,128)}), (f32[1024,128]{1,0:T(8,128)}, f32[1024,128]{1,0:T(8,128)}, f32[1024,256]{1,0:T(8,128)})) %all-reduce.10.cloned.1.call-update) | async-done | bytes 2097168 | tf_op jit(solution)/shard_map/psum | solution.py:754
  319.9 236.4 %all-reduce.12.cloned.1.call-done = (bf16[1024,256]{1,0:T(8,128)(2,1)}, bf16[1024,768]{1,0:T(8,128)(2,1)}, bf16[1024,768]{1,0:T(8,128)(2,1)}, bf16[256,1024]{1,0...) async-done(((bf16[1024,256]{1,0:T(8,128)(2,1)}, bf16[1024,768]{1,0:T(8,128)(2,1)}, ...) | async-done | bytes 12058640 | tf_op jit(solution)/shard_map/psum | solution.py:749
  (279 shorter events, 99.2 us)
Async XLA Ops:
  7.3 310.4 %all-reduce.10.cloned.1.call-start = ((), (), s32[]{:S(2)}) async-start(), calls=%async_computation | async-start | bytes 4194304 | tf_op jit(solution)/shard_map/psum | solution.py:754
  7.3 20.2 %collective-permute-start = (s32[1]{0:T(128)}, s32[1]{0:T(128)}, u32[]{:S(2)}, u32[]{:S(2)}) collective-permute-start(s32[1]{0:T(128)} %param.27), channel_id=1, source_target_pairs={{1,0},{0,1},{3,2},{2,3},{5,4},{4,5},{7,6},{6,7},{9,8},{8,9},{11,10... | collective-permute-start | bytes 20 | tf_op jit(solution)/shard_map/ppermute | solution.py:550
  12.2 61.4 %collective-permute-start.6 = (bf16[256,1024]{1,0:T(8,128)(2,1)S(1)}, bf16[256,1024]{1,0:T(8,128)(2,1)}, u32[]{:S(2)}, u32[]{:S(2)}) collective-permute-start(bf16[256,1024]{1,0:T(8,128)(2,1)S(1)} %broadcast_select_fusion.ct_ref), channel_id=1, source_target_pairs={{1,0},{0,1},{3,2},{2,3},{5,4},{4,5},{7,6},{6,7},{9,8},{8,9},{11,10... | collective-permute-start | bytes 1572872 | tf_op jit(solution)/shard_map/ppermute | solution.py:550
  14.9 22.2 %collective-permute-start.1 = (bf16[256,1024]{1,0:T(8,128)(2,1)S(1)}, bf16[256,1024]{1,0:T(8,128)(2,1)S(1)}, u32[]{:S(2)}, u32[]{:S(2)}) collective-permute-start(bf16[256,1024]{1,0:T(8,128)(2,1)S(1)} %fusion.2.h_ref), channel_id=1, source_target_pairs={{1,0},{0,1},{3,2},{2,3},{5,4},{4,5},{7,6},{6,7},{9,8},{8,9},{11,10... | collective-permute-start | bytes 1572872 | tf_op jit(solution)/shard_map/ppermute | solution.py:550
  27.5 16.7 %copy-start.53 = (f32[256,256]{1,0:T(8,128)}, f32[256,256]{1,0:T(8,128)S(1)}, u32[]{:S(2)}) copy-start(f32[256,256]{1,0:T(8,128)S(1)} %get-tuple-element.108.bcp_ref) | copy-start | bytes 786436
  27.5 92.3 %copy-start.44 = (f32[256,768]{1,0:T(8,128)}, f32[256,768]{1,0:T(8,128)S(1)}, u32[]{:S(2)}) copy-start(f32[256,768]{1,0:T(8,128)S(1)} %get-tuple-element.92.z_ref) | copy-start | bytes 2359300
  27.5 18.4 %collective-permute-start.3 = (f32[16,256]{1,0:T(8,128)S(1)}, f32[16,256]{1,0:T(8,128)S(1)}, u32[]{:S(2)}, u32[]{:S(2)}) collective-permute-start(f32[16,256]{1,0:T(8,128)S(1)} %get-tuple-element.93), channel_id=1, source_target_pairs={{1,0},{0,1},{3,2},{2,3},{5,4},{4,5},{7,6},{6,7},{9,8},{8,9},{11,10... | collective-permute-start | bytes 49160 | tf_op jit(solution)/shard_map/ppermute | solution.py:550
  45.6 84.8 %copy-start.47 = (f32[256,768]{1,0:T(8,128)}, f32[256,768]{1,0:T(8,128)S(1)}, u32[]{:S(2)}) copy-start(f32[256,768]{1,0:T(8,128)S(1)} %get-tuple-element.101.z_ref) | copy-start | bytes 2359300
  45.6 20.6 %collective-permute-start.2 = (f32[16,256]{1,0:T(8,128)S(1)}, f32[16,256]{1,0:T(8,128)S(1)}, u32[]{:S(2)}, u32[]{:S(2)}) collective-permute-start(f32[16,256]{1,0:T(8,128)S(1)} %get-tuple-element.94), channel_id=1, source_target_pairs={{1,0},{0,1},{3,2},{2,3},{5,4},{4,5},{7,6},{6,7},{9,8},{8,9},{11,10... | collective-permute-start | bytes 49160 | tf_op jit(solution)/shard_map/ppermute | solution.py:550
  51.1 15.0 %copy-start.26 = (bf16[256,768]{1,0:T(8,128)(2,1)}, bf16[256,768]{1,0:T(8,128)(2,1)S(1)}, u32[]{:S(2)}) copy-start(bf16[256,768]{1,0:T(8,128)(2,1)S(1)} %get-tuple-element.142) | copy-start | bytes 1179652
  51.1 19.3 %collective-permute-start.4 = (bf16[256,1024]{1,0:T(8,128)(2,1)S(1)}, bf16[256,1024]{1,0:T(8,128)(2,1)S(1)}, u32[]{:S(2)}, u32[]{:S(2)}) collective-permute-start(bf16[256,1024]{1,0:T(8,128)(2,1)S(1)} %get-tuple-element.102), channel_id=1, source_target_pairs={{0,1},{1,0},{2,3},{3,2},{4,5},{5,4},{6,7},{7,6},{8,9},{9,8},{10,11... | collective-permute-start | bytes 1572872 | tf_op jit(solution)/shard_map/ppermute | solution.py:553
  52.9 13.2 %copy-start.45 = (f32[256,768]{1,0:T(8,128)S(1)}, f32[256,768]{1,0:T(8,128)}, u32[]{:S(2)}) copy-start(f32[256,768]{1,0:T(8,128)} %get-tuple-element.91.x_ref) | copy-start | bytes 2359300
  52.9 13.2 %copy-start.46 = (f32[256,768]{1,0:T(8,128)S(1)}, f32[256,768]{1,0:T(8,128)}, u32[]{:S(2)}) copy-start(f32[256,768]{1,0:T(8,128)} %get-tuple-element.90.y_ref) | copy-start | bytes 2359300
  73.2 11.8 %collective-permute-start.5 = (bf16[256,1024]{1,0:T(8,128)(2,1)S(1)}, bf16[256,1024]{1,0:T(8,128)(2,1)S(1)}, u32[]{:S(2)}, u32[]{:S(2)}) collective-permute-start(bf16[256,1024]{1,0:T(8,128)(2,1)S(1)} %multiply_convert_fusion.h_ref), channel_id=1, source_target_pairs={{1,0},{0,1},{3,2},{2,3},{5,4},{4,5},{7,6},{6,7},{9,8},{8,9},{11,10... | collective-permute-start | bytes 1572872 | tf_op jit(solution)/shard_map/ppermute | solution.py:550
  94.1 13.7 %collective-permute-start.8 = (bf16[256,1024]{1,0:T(8,128)(2,1)S(1)}, bf16[256,1024]{1,0:T(8,128)(2,1)}, u32[]{:S(2)}, u32[]{:S(2)}) collective-permute-start(bf16[256,1024]{1,0:T(8,128)(2,1)S(1)} %get-tuple-element.106), channel_id=1, source_target_pairs={{0,1},{1,0},{2,3},{3,2},{4,5},{5,4},{6,7},{7,6},{8,9},{9,8},{10,11... | collective-permute-start | bytes 1572872 | tf_op jit(solution)/shard_map/ppermute | solution.py:553
  102.6 13.5 %collective-permute-start.7 = (bf16[256,1024]{1,0:T(8,128)(2,1)S(1)}, bf16[256,1024]{1,0:T(8,128)(2,1)S(1)}, u32[]{:S(2)}, u32[]{:S(2)}) collective-permute-start(bf16[256,1024]{1,0:T(8,128)(2,1)S(1)} %get-tuple-element.104), channel_id=1, source_target_pairs={{0,1},{1,0},{2,3},{3,2},{4,5},{5,4},{6,7},{7,6},{8,9},{9,8},{10,11... | collective-permute-start | bytes 1572872 | tf_op jit(solution)/shard_map/ppermute | solution.py:553
  118.9 11.5 %collective-permute-start.9 = (bf16[256,1024]{1,0:T(8,128)(2,1)S(1)}, bf16[256,1024]{1,0:T(8,128)(2,1)S(1)}, u32[]{:S(2)}, u32[]{:S(2)}) collective-permute-start(bf16[256,1024]{1,0:T(8,128)(2,1)S(1)} %get-tuple-element.178.db_ref), channel_id=1, source_target_pairs={{1,0},{0,1},{3,2},{2,3},{5,4},{4,5},{7,6},{6,7},{9,8},{8,9},{11,10... | collective-permute-start | bytes 1572872 | tf_op jit(solution)/shard_map/ppermute | solution.py:550
  122.7 14.7 %collective-permute-start.11 = (f32[16,256]{1,0:T(8,128)S(1)}, f32[16,256]{1,0:T(8,128)S(1)}, u32[]{:S(2)}, u32[]{:S(2)}) collective-permute-start(f32[16,256]{1,0:T(8,128)S(1)} %get-tuple-element.112), channel_id=1, source_target_pairs={{1,0},{0,1},{3,2},{2,3},{5,4},{4,5},{7,6},{6,7},{9,8},{8,9},{11,10... | collective-permute-start | bytes 49160 | tf_op jit(solution)/shard_map/ppermute | solution.py:550
  133.5 29.4 %collective-permute-start.10 = (f32[16,256]{1,0:T(8,128)S(1)}, f32[16,256]{1,0:T(8,128)S(1)}, u32[]{:S(2)}, u32[]{:S(2)}) collective-permute-start(f32[16,256]{1,0:T(8,128)S(1)} %get-tuple-element.113), channel_id=1, source_target_pairs={{1,0},{0,1},{3,2},{2,3},{5,4},{4,5},{7,6},{6,7},{9,8},{8,9},{11,10... | collective-permute-start | bytes 49160 | tf_op jit(solution)/shard_map/ppermute | solution.py:550
  168.5 11.7 %copy-start.16 = (bf16[256,256]{1,0:T(8,128)(2,1)S(1)}, bf16[256,256]{1,0:T(8,128)(2,1)}, u32[]{:S(2)}) copy-start(bf16[256,256]{1,0:T(8,128)(2,1)} %copy-done.15) | copy-start | bytes 393220
  181.7 374.5 %all-reduce.12.cloned.1.call-start = ((), (), s32[]{:S(2)}) async-start(), calls=%async_computation.1 | async-start | bytes 24117248 | tf_op jit(solution)/shard_map/psum | solution.py:749
  197.7 65.2 %copy-start.66 = (bf16[256,1024]{1,0:T(8,128)(2,1)S(1)}, bf16[256,1024]{1,0:T(8,128)(2,1)}, u32[]{:S(2)}) copy-start(bf16[256,1024]{1,0:T(8,128)(2,1)} %param.26) | copy-start | bytes 1572868
  197.7 65.2 %copy-start.79 = (f32[1024]{0:T(1024)S(1)}, f32[1024]{0:T(1024)}, u32[]{:S(2)}) copy-start(f32[1024]{0:T(1024)} %param.29) | copy-start | bytes 12292
  198.7 64.2 %collective-permute-start.12 = (bf16[256,1024]{1,0:T(8,128)(2,1)S(1)}, bf16[256,1024]{1,0:T(8,128)(2,1)S(1)}, u32[]{:S(2)}, u32[]{:S(2)}) collective-permute-start(bf16[256,1024]{1,0:T(8,128)(2,1)S(1)} %copy-done.5), channel_id=1, source_target_pairs={{0,1},{1,0},{2,3},{3,2},{4,5},{5,4},{6,7},{7,6},{8,9},{9,8},{10,11... | collective-permute-start | bytes 1572872 | tf_op jit(solution)/shard_map/ppermute | solution.py:553
  (77 other events, 260.8 us)
Sparse Core Ops, SparseCore 0:
  181.8 135.7 all-reduce.9
  325.9 230.3 all-reduce.11
